TPU v7x, 128 devices: a whole 4x4x4 slice. The times are simulated.
128 devices in a mesh: group: 4 (over y), shard: 32 (over z, x, core).
Axes of the slice: x: 4, y: 4, z: 4, core: 2. Of those that a mesh axis runs over, the one named last changes fastest.
Arguments:
- tokens: bfloat16 [128, 192, 768], P(('group', 'shard')), may hold values from -650 to 650
- norm_gain: float32 [768], replicated, may hold values from 0.1 to 1.9
- w_query: bfloat16 [768, 768], P('shard'), may hold values from -8 to 8
- w_key: bfloat16 [768, 768], P('shard'), may hold values from -0.21875 to 0.21875
- w_value: bfloat16 [768, 768], P('shard'), may hold values from -0.625 to 0.625
- w_out: bfloat16 [768, 768], P('shard'), may hold values from -0.21875 to 0.21875
- owner_map: int32 [4, 32], P('group'), may hold values from 0 to 31, each once within a row
- pair_images: int32 [1024, 2], P(('group', 'shard')), may hold values from 0 to 31, as said below
- pair_count: int32 [128], P(('group', 'shard')), may hold values from 1 to 8, 512 in all
- confidence: int32 [1024, 2], P(('group', 'shard')), may hold values from 1 to 8
Outputs:
- updated: bfloat16 [128, 192, 768], P(('group', 'shard'))
Inputs may be any that keep to these rules, and one draw needn't show every extreme that they name: `pair_images`: each row names two different images of the listing device's own group, by their index within that group. Device d lists its pairs in its first pair_count[d] rows of pair_images and confidence; the other rows are unused.
All inputs are finite; a program needn't handle non-finite values.
Results may differ from a plain program's by a relative error of at most 0.013.
The roundings to bfloat16 on the way count: a program that leaves them out, or rounds other values in their place, can miss the bound.
Values may be sent and summed in bfloat16 or wider, within the bound.
A program may use at most 128 MiB of HBM per device.

v0:
```python
import math

import jax
import jax.numpy as jnp
from jax import lax
from jax.sharding import PartitionSpec as P

HEADS = 12
HEAD_DIM = 64


def layer_norm(values, norm_gain):
    values = values.astype(jnp.float32)
    average = jnp.mean(values, axis=-1, keepdims=True)
    centred = values - average
    variance = jnp.mean(centred * centred, axis=-1, keepdims=True)
    return (centred * lax.rsqrt(variance + 1e-05) * norm_gain).astype(jnp.bfloat16)


def attend_many(queries, keys_many, values_many, out_weight):
    count = queries.shape[0]
    length = queries.shape[1]
    query_heads = queries.reshape(count, length, HEADS, HEAD_DIM)
    key_heads = keys_many.reshape(count, length, HEADS, HEAD_DIM)
    value_heads = values_many.reshape(count, length, HEADS, HEAD_DIM)
    scores = jnp.einsum(
        "bqhd,bkhd->bhqk", query_heads, key_heads, preferred_element_type=jnp.float32
    )
    scores = scores * (1.0 / math.sqrt(HEAD_DIM))
    scores = scores - jnp.max(scores, axis=-1, keepdims=True)
    expo = jnp.exp(scores)
    attention = (expo / jnp.sum(expo, axis=-1, keepdims=True)).astype(jnp.bfloat16)
    attended = jnp.einsum(
        "bhqk,bkhd->bqhd", attention, value_heads, preferred_element_type=jnp.float32
    )
    attended = attended.reshape(count * length, HEADS * HEAD_DIM).astype(jnp.bfloat16)
    projected = jnp.dot(attended, out_weight, preferred_element_type=jnp.float32)
    return projected.reshape(count, length, HEADS * HEAD_DIM)


def project_rows(rows, weight):
    return jnp.dot(rows, weight, preferred_element_type=jnp.float32).astype(jnp.bfloat16)


def shards(
    tokens,
    norm_gain,
    w_query,
    w_key,
    w_value,
    w_out,
    owner_map,
    pair_images,
    pair_count,
    confidence,
):
    normed = layer_norm(tokens[0], norm_gain)
    query_weight, key_weight, value_weight, out_weight = (
        lax.all_gather(w_query, "shard", axis=0, tiled=True),
        lax.all_gather(w_key, "shard", axis=0, tiled=True),
        lax.all_gather(w_value, "shard", axis=0, tiled=True),
        lax.all_gather(w_out, "shard", axis=0, tiled=True),
    )
    owners = owner_map[0]
    shard_total = lax.axis_size("shard")
    length = normed.shape[0]
    width = normed.shape[1]
    every_image = lax.all_gather(normed[None], "shard", axis=0, tiled=True)

    def fetch_query(stored):
        return project_rows(every_image[stored], query_weight)

    def fetch_pair(stored):
        picture = every_image[stored]
        return (project_rows(picture, key_weight), project_rows(picture, value_weight))

    pair_total = pair_count[0]

    def one_pair(number, carried):
        numerator, weight_total = carried
        store_first = owners[pair_images[number, 0]]
        store_second = owners[pair_images[number, 1]]
        first_query = fetch_query(store_first)
        second_query = fetch_query(store_second)
        first_key, first_value = fetch_pair(store_first)
        second_key, second_value = fetch_pair(store_second)
        queries = jnp.stack([first_query, second_query])
        keys_both = jnp.stack([second_key, first_key])
        values_both = jnp.stack([second_value, first_value])
        projected = attend_many(queries, keys_both, values_both, out_weight)
        first_weight = confidence[number, 0].astype(jnp.float32)
        second_weight = confidence[number, 1].astype(jnp.float32)
        numerator = numerator.at[store_first].add(first_weight * projected[0])
        numerator = numerator.at[store_second].add(second_weight * projected[1])
        weight_total = weight_total.at[store_first].add(first_weight)
        weight_total = weight_total.at[store_second].add(second_weight)
        return (numerator, weight_total)

    start = (
        jnp.zeros((shard_total, length, width), jnp.float32),
        jnp.zeros((shard_total,), jnp.float32),
    )
    numerator, weight_total = lax.fori_loop(0, pair_total, one_pair, start)
    summed, totals = (
        lax.psum_scatter(
            numerator.astype(jnp.bfloat16), "shard", scatter_dimension=0, tiled=True
        ).astype(jnp.float32),
        lax.psum_scatter(
            weight_total.astype(jnp.bfloat16), "shard", scatter_dimension=0, tiled=True
        ).astype(jnp.float32),
    )
    return (summed / (1.0 + totals)[:, None, None]).astype(jnp.bfloat16)


def solution(mesh):
    in_specs = (
        P(("group", "shard"), None, None),
        P(),
        P("shard", None),
        P("shard", None),
        P("shard", None),
        P("shard", None),
        P("group", None),
        P(("group", "shard"), None),
        P(("group", "shard")),
        P(("group", "shard"), None),
    )
    out_specs = P(("group", "shard"), None, None)
    return jax.shard_map(shards, mesh=mesh, in_specs=in_specs, out_specs=out_specs, check_vma=False)
```

profile of v0, /device:TPU:1, one launch (start us, length us, event | category | flops | bytes accessed | tf_op | source)
XLA Modules:
  0.0 831.9 jit_solution(3613127525899226354)
XLA Ops:
  13.6 42.8 %all-gather.10.cloned.1.call-done = bf16[768,768]{1,0:T(8,128)(2,1)} async-done(((bf16[24,768]{1,0:T(8,128)(2,1)}), bf16[768,768]{1,0:T(8,128)(2,1)}) %all-gather.10.cloned.1.call-update) | async-done | bytes 1179664 | tf_op jit(solution)/shard_map/all_gather | solution.py:59
  56.4 44.6 %all-gather.12.cloned.1.call-done = bf16[768,768]{1,0:T(8,128)(2,1)} async-done(((bf16[24,768]{1,0:T(8,128)(2,1)}), bf16[768,768]{1,0:T(8,128)(2,1)}) %all-gather.12.cloned.1.call-update) | async-done | bytes 1179664 | tf_op jit(solution)/shard_map/all_gather | solution.py:60
  101.1 44.7 %all-gather.14.cloned.1.call-done = bf16[768,768]{1,0:T(8,128)(2,1)} async-done(((bf16[24,768]{1,0:T(8,128)(2,1)}), bf16[768,768]{1,0:T(8,128)(2,1)}) %all-gather.14.cloned.1.call-update) | async-done | bytes 1179664 | tf_op jit(solution)/shard_map/all_gather | solution.py:62
  145.7 44.5 %all-gather.8.cloned.1.call-done = bf16[768,768]{1,0:T(8,128)(2,1)} async-done(((bf16[24,768]{1,0:T(8,128)(2,1)}), bf16[768,768]{1,0:T(8,128)(2,1)}) %all-gather.8.cloned.1.call-update) | async-done | bytes 1179664 | tf_op jit(solution)/shard_map/all_gather | solution.py:61
  190.2 56.9 %all-gather.6.cloned.1.call-done = bf16[32,192,768]{2,1,0:T(8,128)(2,1)} async-done(((bf16[1,192,768]{2,1,0:T(8,128)(2,1)}), bf16[32,192,768]{2,1,0:T(8,128)(2,1)}) %all-gather.6.cloned.1.call-update) | async-done | bytes 9437200 | tf_op jit(solution)/shard_map/all_gather | solution.py:68
  247.1 8.7 %broadcast_in_dim.4 = f32[32,192,768]{2,1,0:T(8,128)} broadcast(f32[]{:T(128)} %constant.103.clone.1), dimensions={} | broadcast | bytes 18874372 | tf_op jit(solution)/shard_map/broadcast_in_dim | solution.py:100
  255.8 174.7 %while.16 = (s32[]{:T(128)}, f32[32,192,768]{2,1,0:T(8,128)}, f32[32]{0:T(128)S(1)}, s32[]{:T(128)}, s32[8,2]{0,1:T(2,128)S(1)}, /*index=5*/s32[32]{0:T(128)S(1)...) while((s32[]{:T(128)}, f32[32,192,768]{2,1,0:T(8,128)}, ...), condition=%wide.region_7.8_spmd, body=%wide.region_2.7_spmd.sunk | while | flops 2046689536 | bytes 39562184 | solution.py:103
  281.5 2.2 fusion.106
  283.7 4.0 fusion.107
  295.6 3.1 fusion.108
  300.5 3.0 convert_element_type.128
  303.5 2.1 fusion.109
  307.6 2.6 fusion.110
  310.9 2.6 fusion.111
  339.6 2.2 fusion.106
  341.7 4.0 fusion.107
  353.7 3.1 fusion.108
  358.5 3.0 convert_element_type.128
  361.6 2.1 fusion.109
  365.7 2.7 fusion.110
  369.0 2.6 fusion.111
  379.8 2.1 convolution_convert_fusion.12
  397.6 2.2 fusion.106
  399.8 4.0 fusion.107
  411.7 3.1 fusion.108
  416.6 3.0 convert_element_type.128
  419.6 2.1 fusion.109
  423.7 2.6 fusion.110
  427.0 2.6 fusion.111
  430.6 9.8 %convert_element_type.71 = bf16[32,192,768]{2,1,0:T(8,128)(2,1)} convert(f32[32,192,768]{2,1,0:T(8,128)} %get-tuple-element.117) | non-fusion elementwise | flops 4718592 | bytes 28311552 | tf_op jit(solution)/shard_map/convert_element_type | solution.py:106
  441.7 350.1 %all-reduce = bf16[32]{0:T(256)(128)(2,1)S(1)} all-reduce(bf16[32]{0:T(256)(128)(2,1)S(1)} %convert_element_type.73), channel_id=3, replica_groups=mesh['group'=4,'shard'=32] {'shard'}, use_global_device_ids=true, to_apply=%region_9.0.clone | all-reduce | flops 32 | bytes 128
  793.8 29.5 %reduce-scatter.2.cloned.1.call-done = bf16[1,192,768]{2,1,0:T(8,128)(2,1)} async-done(((bf16[32,192,768]{2,1,0:T(8,128)(2,1)}), bf16[1,192,768]{2,1,0:T(8,128)(2,1)}) %reduce-scatter.2.cloned.1.call-update) | async-done | bytes 294928 | tf_op jit(solution)/shard_map/reduce_scatter | solution.py:105
  (89 shorter events, 94.9 us)
Async XLA Ops:
  6.5 49.9 %all-gather.10.cloned.1.call-start = ((), (), s32[]{:S(2)}) async-start(), calls=%async_computation.3 | async-start | bytes 1216512 | tf_op jit(solution)/shard_map/all_gather | solution.py:59
  7.3 93.8 %all-gather.12.cloned.1.call-start = ((), (), s32[]{:S(2)}) async-start(), calls=%async_computation.4 | async-start | bytes 1216512 | tf_op jit(solution)/shard_map/all_gather | solution.py:60
  8.0 137.7 %all-gather.14.cloned.1.call-start = ((), (), s32[]{:S(2)}) async-start(), calls=%async_computation.5 | async-start | bytes 1216512 | tf_op jit(solution)/shard_map/all_gather | solution.py:62
  8.7 181.5 %all-gather.8.cloned.1.call-start = ((), (), s32[]{:S(2)}) async-start(), calls=%async_computation.2 | async-start | bytes 1216512 | tf_op jit(solution)/shard_map/all_gather | solution.py:61
  9.3 237.8 %all-gather.6.cloned.1.call-start = ((), (), s32[]{:S(2)}) async-start(), calls=%async_computation.1 | async-start | bytes 9732096 | tf_op jit(solution)/shard_map/all_gather | solution.py:68
  13.6 809.8 %reduce-scatter.2.cloned.1.call-start = ((), (), s32[]{:S(2)}) async-start(), calls=%async_computation.6 | async-start | bytes 9732096 | tf_op jit(solution)/shard_map/reduce_scatter | solution.py:105
  247.1 8.7 %copy-start = (bf16[768,768]{1,0:T(8,128)(2,1)S(1)}, bf16[768,768]{1,0:T(8,128)(2,1)}, u32[]{:S(2)}) copy-start(bf16[768,768]{1,0:T(8,128)(2,1)} %all-gather.10.cloned.1.call-done) | copy-start | bytes 3538948
  247.1 8.7 %copy-start.1 = (bf16[768,768]{1,0:T(8,128)(2,1)S(1)}, bf16[768,768]{1,0:T(8,128)(2,1)}, u32[]{:S(2)}) copy-start(bf16[768,768]{1,0:T(8,128)(2,1)} %all-gather.12.cloned.1.call-done) | copy-start | bytes 3538948
  247.1 8.7 %copy-start.2 = (bf16[768,768]{1,0:T(8,128)(2,1)S(1)}, bf16[768,768]{1,0:T(8,128)(2,1)}, u32[]{:S(2)}) copy-start(bf16[768,768]{1,0:T(8,128)(2,1)} %all-gather.8.cloned.1.call-done) | copy-start | bytes 3538948
  247.1 8.7 %copy-start.3 = (s32[1,32]{1,0:T(1,128)S(1)}, s32[1,32]{1,0:T(1,128)}, u32[]{:S(2)}) copy-start(s32[1,32]{1,0:T(1,128)} %param.26) | copy-start | bytes 388
  247.1 8.7 %copy-start.4 = (s32[8,2]{0,1:T(2,128)S(1)}, s32[8,2]{0,1:T(2,128)}, u32[]{:S(2)}) copy-start(s32[8,2]{0,1:T(2,128)} %param.27) | copy-start | bytes 196
  247.1 8.7 %copy-start.5 = (s32[8,2]{0,1:T(2,128)S(1)}, s32[8,2]{0,1:T(2,128)}, u32[]{:S(2)}) copy-start(s32[8,2]{0,1:T(2,128)} %param.29) | copy-start | bytes 196
  440.4 0.7 copy-start.6
Sparse Core Ops, SparseCore 0:
  9.7 46.6 all-gather.9
  58.7 42.2 all-gather.11
  103.4 42.2 all-gather.13
  147.9 42.2 all-gather.7
  192.3 54.7 all-gather.5
  440.6 382.7 reduce-scatter.1
where the time goes:
time: 839 us; the launch traced here: 832 us
  blocking collectives  350 us (42%)
  waiting for transfers between devices  266 us (32%)
  local copies, waits for them, and re-layouts  63.3 us (8%)
  matrix products  59.8 us (7%)
  other arithmetic  48.8 us (6%)
  loops' own time  29.8 us (4%)
  between operations  14.3 us (2%)
    unnamed x1, blocking collectives  350 us
    all_gather x1, waiting for transfers between devices, shards(): every_image = lax.all_gather(normed[None], 'shard', axis=0, tiled=True)  56.9 us
    all_gather x1, waiting for transfers between devices, shards(): lax.all_gather(w_out, 'shard', axis=0, tiled=True)  44.7 us
    all_gather x1, waiting for transfers between devices, shards(): lax.all_gather(w_key, 'shard', axis=0, tiled=True)  44.6 us
    all_gather x1, waiting for transfers between devices, shards(): lax.all_gather(w_value, 'shard', axis=0, tiled=True)  44.5 us
    all_gather x1, waiting for transfers between devices, shards(): lax.all_gather(w_query, 'shard', axis=0, tiled=True)  42.8 us
    dot_general x18, matrix products, project_rows(): jnp.dot(rows, weight, preferred_element_type=jnp.float32)  37.5 us
    convert_element_type x18, local copies, waits for them, and re-layouts, project_rows(): jnp.dot(rows, weight, preferred_element_type=jnp.float32)  34 us
  transfers between devices with their start and end apart: 6, of which 6 were waited for; matrix products, arithmetic and copies ran while one was open for 1% of the time, Pallas kernels for 0%

commit v1 on v0

v1 whole, which is shorter than its diff:
```python
import math

import jax
import jax.numpy as jnp
from jax import lax
from jax.experimental import pallas as pl
from jax.experimental.pallas import tpu as pltpu
from jax.sharding import PartitionSpec as P

MESH = pl.DeviceIdType.MESH
F32, BF16, I32 = jnp.float32, jnp.bfloat16, jnp.int32
SEQ, D, RING, PLANE = 192, 768, 4, 16
WIDE = 192
ROWS = 24
NT = (((1,), (1,)), ((), ()))
TN = (((0,), (0,)), ((), ()))
FIRST = (0, 3, 1, 2)


def place():
    shard = lax.axis_index("shard")
    core = lax.rem(shard, 2)
    chip = lax.div(shard, 2)
    return lax.rem(chip, RING), lax.div(chip, RING), core


def device(x, z, core):
    return {"shard": (z * RING + x) * 2 + core}


def gather_kernel(
    tok, gain, wq, wk, wv, wo, omap, pimg, pcnt, conf,
    kv, qt, weights, total, wo_all,
    img, staged, wplane, woplane, lists, wt, send, recv, pair_send, pair_recv,
):
    x, z, core = place()
    chip = z * RING + x

    def turn(value, offset):
        return lax.rem(value + offset, RING)

    def slot(ox, oz):
        return turn(z, oz) * RING + turn(x, ox)

    sibling = device(x, z, 1 - core)
    barrier = pltpu.get_barrier_semaphore()
    for offset in (1, 2, 3):
        pl.semaphore_signal(barrier, 1, device_id=device(turn(x, offset), z, core), device_id_type=MESH)
        pl.semaphore_signal(barrier, 1, device_id=device(x, turn(z, offset), core), device_id_type=MESH)
    pl.semaphore_signal(barrier, 1, device_id=sibling, device_id_type=MESH)

    parts = [w[...].astype(F32) for w in (wq, wk, wv)]
    for g in range(RING):
        cols = [w[:, g * WIDE:(g + 1) * WIDE] for w in parts] + [jnp.zeros((ROWS, 64), F32)]
        slice_g = jnp.concatenate(cols, axis=1)
        staged[g] = jnp.concatenate([slice_g, jnp.zeros((8, 640), F32)], axis=0).astype(BF16)
    wplane[core, chip] = staged[x]
    woplane[core, chip] = jnp.concatenate(
        [wo[...].astype(F32), jnp.zeros((8, D), F32)], axis=0
    ).astype(BF16)
    lane32 = lax.broadcasted_iota(I32, (8, 32), 1)

    def stored(column):
        return jnp.sum(jnp.where(pimg[:, column:column + 1] == lane32, omap[...], 0), axis=1, keepdims=True)

    lane = lax.broadcasted_iota(I32, (8, 128), 1)
    listed = lax.broadcasted_iota(I32, (8, 128), 0) < pcnt[...]
    lists[core, chip] = jnp.where(
        lane == 0, stored(0),
        jnp.where(
            lane == 1, stored(1),
            jnp.where(
                lane == 2, jnp.where(listed, conf[:, 0:1], 0),
                jnp.where(lane == 3, jnp.where(listed, conf[:, 1:2], 0), 0),
            ),
        ),
    )
    values = tok[0].astype(F32)
    centred = values - jnp.mean(values, axis=-1, keepdims=True)
    variance = jnp.mean(centred * centred, axis=-1, keepdims=True)
    img[chip] = (centred * lax.rsqrt(variance + 1e-05) * gain[...]).astype(BF16)

    pl.semaphore_wait(barrier, 7)

    started = []

    def copy(source, target, number, where):
        return pltpu.make_async_remote_copy(
            src_ref=source, dst_ref=target, send_sem=send.at[number], recv_sem=recv.at[number],
            device_id=where, device_id_type=MESH,
        )

    def start(source, target, number, where):
        one = copy(source, target, number, where)
        one.start()
        started.append(one)

    def arrived(target, number):
        copy(target, target, number, sibling).wait_recv()

    def along_x(buffer, base, outgoing=None):
        for offset in (1, 2, 3):
            block = buffer.at[core, chip]
            source = block if outgoing is None else outgoing.at[turn(x, offset)]
            start(source, block, base + offset - 1, device(turn(x, offset), z, core))

    def along_z(buffer, base):
        for offset in (1, 2, 3):
            arrived(buffer.at[core, z * RING + turn(x, 4 - offset)], base + offset - 1)
        for offset in (1, 2, 3):
            row = buffer.at[core, pl.ds(z * RING, RING)]
            start(row, row, base + 2 + offset, device(x, turn(z, offset), core))

    def across(buffer, base):
        for offset in (1, 2, 3):
            arrived(buffer.at[core, pl.ds(turn(z, 4 - offset) * RING, RING)], base + 2 + offset)
        start(buffer.at[core], buffer.at[core], base + 6, sibling)

    def ended(buffer, base):
        arrived(buffer.at[1 - core], base + 6)

    def piece(half, first, second, part=None):
        low, count = (96 * half, 96) if part is None else (96 * half + 48 * part, 48)
        where = slot(first, second) if half == 0 else slot(second, first)
        return img.at[where, pl.ds(low, count)]

    def neighbour(axis, direction):
        step = 1 if direction == 0 else 3
        return device(turn(x, step), z, core) if axis == 0 else device(x, turn(z, step), core)

    def first_ring(half, direction):
        start(piece(half, 0, 0), piece(half, 0, 0), 20 * half + direction, neighbour(half, direction))

    def first_forward(half, direction):
        block = piece(half, (3, 1)[direction], 0, direction)
        start(block, block, 20 * half + 2 + direction, neighbour(half, direction))

    def second_ring(half, k):
        for direction in (0, 1):
            block = piece(half, FIRST[k], 0)
            start(block, block, 20 * half + 4 + 4 * k + direction, neighbour(1 - half, direction))

    def second_forward(half, k, direction):
        block = piece(half, FIRST[k], (3, 1)[direction], direction)
        start(block, block, 20 * half + 6 + 4 * k + direction, neighbour(1 - half, direction))

    def got_first(half, direction):
        arrived(piece(half, (3, 1)[direction], 0), 20 * half + direction)

    def got_first_forward(half, direction):
        arrived(piece(half, 2, 0, direction), 20 * half + 2 + direction)

    def got_second(half, k, direction):
        arrived(piece(half, FIRST[k], (3, 1)[direction]), 20 * half + 4 + 4 * k + direction)

    def got_second_forward(half, k, direction):
        arrived(piece(half, FIRST[k], 2, direction), 20 * half + 6 + 4 * k + direction)

    def pair_copy(where, row):
        return pltpu.make_async_remote_copy(
            src_ref=kv.at[row], dst_ref=kv.at[row], send_sem=pair_send.at[where],
            recv_sem=pair_recv.at[where], device_id=sibling, device_id_type=MESH,
        )

    def project(count, offsets):
        def one(i, carried):
            where = slot(*offsets(i))
            row = where * 2 + core
            normed = img[where]
            kv[row, 0:WIDE, :] = lax.dot_general(
                normed, wt[WIDE:2 * WIDE, :], NT, preferred_element_type=F32
            ).astype(BF16)
            kv[row, WIDE:2 * WIDE, :] = lax.dot_general(
                wt[2 * WIDE:3 * WIDE, :], normed, NT, preferred_element_type=F32
            ).astype(BF16)
            pair_copy(where, row).start()
            return carried

        lax.fori_loop(0, count, one, 0)

    W0, L0, O0 = 40, 47, 54
    along_x(wplane, W0, staged)
    along_x(lists, L0)
    for half in (0, 1):
        for direction in (0, 1):
            first_ring(half, direction)
        second_ring(half, 0)
    along_z(wplane, W0)
    along_z(lists, L0)

    for direction in (0, 1):
        for half in (0, 1):
            got_first(half, direction)
            first_forward(half, direction)
            second_ring(half, 1 + direction)
    for direction in (0, 1):
        for half in (0, 1):
            got_second(half, 0, direction)
            second_forward(half, 0, direction)
    across(wplane, W0)
    across(lists, L0)
    along_x(woplane, O0)
    ended(wplane, W0)
    ended(lists, L0)

    for j in (0, 1):
        blocks = []
        for one in range(8 * j, 8 * j + 8):
            for c in (0, 1):
                blocks.append(wplane[c, one].astype(F32)[0:ROWS, :])
        wt[:, 384 * j:384 * (j + 1)] = jnp.concatenate(blocks, axis=0).T.astype(BF16)
    project(1, lambda i: (i, i))
    project(4, lambda i: ((1 + 2 * (i % 2)) * (1 - i // 2), (1 + 2 * (i % 2)) * (i // 2)))

    table = lists[...].reshape(2 * PLANE * 8, 128)
    lanes = lax.broadcasted_iota(I32, (2 * PLANE * 8, 128), 1)
    first, second = table[:, 0:1], table[:, 1:2]
    one_weight, two_weight = table[:, 2:3], table[:, 3:4]
    at_first, at_second = first == lanes, second == lanes

    def weight_row(image):
        taken = jnp.where(at_second, jnp.where(first == image, one_weight, 0), 0)
        taken = taken + jnp.where(at_first, jnp.where(second == image, two_weight, 0), 0)
        return jnp.sum(taken, axis=0, keepdims=True)

    rows = [weight_row((z * RING + i) * 2 + core) for i in range(RING)]
    weights[...] = jnp.concatenate(rows + [jnp.zeros((4, 128), I32)], axis=0)
    own = jnp.sum(weight_row(chip * 2 + core).astype(F32), axis=1, keepdims=True)
    total[...] = jnp.broadcast_to(1.0 + own, (8, 128))

    for half in (0, 1):
        for direction in (0, 1):
            got_first_forward(half, direction)
        second_ring(half, 3)
    for k in (1, 2):
        for direction in (0, 1):
            for half in (0, 1):
                got_second(half, k, direction)
                second_forward(half, k, direction)
    for half in (0, 1):
        for direction in (0, 1):
            got_second_forward(half, 0, direction)
    along_z(woplane, O0)
    project(4, lambda i: (1 + 2 * (i // 2), 1 + 2 * (i % 2)))
    project(2, lambda i: (2 * (1 - i), 2 * i))

    def one_query(i, carried):
        qt[i] = lax.dot_general(
            wt[0:WIDE, :], img[z * RING + i], NT, preferred_element_type=F32
        ).astype(BF16)
        return carried

    lax.fori_loop(0, RING, one_query, 0)

    for direction in (0, 1):
        for half in (0, 1):
            got_second(half, 3, direction)
            second_forward(half, 3, direction)
    for k in (1, 2):
        for direction in (0, 1):
            for half in (0, 1):
                got_second_forward(half, k, direction)
    across(woplane, O0)
    project(4, lambda i: (
        2 * (1 - i // 2) + (1 + 2 * (i % 2)) * (i // 2),
        (1 + 2 * (i % 2)) * (1 - i // 2) + 2 * (i // 2),
    ))
    for half in (0, 1):
        for direction in (0, 1):
            got_second_forward(half, 3, direction)
    project(1, lambda i: (i + 2, i + 2))
    ended(woplane, O0)
    for one in range(PLANE):
        blocks = [woplane[c, one].astype(F32)[0:ROWS, :] for c in (0, 1)]
        wo_all[2 * ROWS * one:2 * ROWS * (one + 1), :] = jnp.concatenate(blocks, axis=0).astype(BF16)

    for one in started:
        one.wait_send()

    def drain(where, carried):
        pair_copy(where, where * 2 + core).wait_send()
        pair_copy(where, where * 2 + 1 - core).wait_recv()
        return carried

    lax.fori_loop(0, PLANE, drain, 0)


WINDOWS = ((0, 256, 0), (128, 384, 64), (384, 576, 0))


def attend_kernel(weights, kv, qt, out, masked, acc, chosen, chosen_weight):
    for i in range(RING):
        masked[i] = jnp.zeros((WIDE, 3 * SEQ), BF16)
        for h in range(3):
            masked[i, 64 * h:64 * (h + 1), SEQ * h:SEQ * (h + 1)] = qt[i, 64 * h:64 * (h + 1), :]
    acc[...] = jnp.zeros_like(acc)

    def note(number, count):
        weight = weights[number // 32, number % 32]
        chosen[count] = number
        chosen_weight[count] = weight
        return count + jnp.where(weight > 0, 1, 0)

    count = lax.fori_loop(0, 128, note, 0, unroll=8)
    chosen[count] = 0
    chosen_weight[count] = 0
    factor = math.log2(math.e) / 8.0

    def direction(entry):
        number = chosen[entry]
        i, t = number // 32, number % 32
        weight = chosen_weight[entry].astype(F32)
        scores = jnp.dot(kv[t, 0:WIDE, :], masked[i], preferred_element_type=F32)
        top = jnp.max(scores, axis=0, keepdims=True)
        expo = jnp.exp2((scores - top) * factor)
        scale = 1.0 / jnp.sum(expo, axis=0, keepdims=True)
        expo = expo.astype(BF16)
        for h, (low, high, _) in enumerate(WINDOWS):
            one = jnp.dot(
                kv[t, WIDE + 64 * h:WIDE + 64 * (h + 1), :], expo[:, low:high],
                preferred_element_type=F32,
            )
            one = (one * scale[:, low:high]).astype(BF16).astype(F32) * weight
            acc[i, h, :, 0:high - low] += one

    def two(number, carried):
        direction(2 * number)
        direction(2 * number + 1)
        return carried

    lax.fori_loop(0, (count + 1) // 2, two, 0)
    for i in range(RING):
        for h, (_, _, low) in enumerate(WINDOWS):
            out[i, 64 * h:64 * (h + 1), :] = acc[i, h][:, low:low + SEQ].astype(BF16)


def output_kernel(attended, wo_all, total, out, held, send, recv):
    x, z, core = place()
    barrier = pltpu.get_barrier_semaphore()
    for offset in (1, 2, 3):
        pl.semaphore_signal(
            barrier, 1, device_id=device(lax.rem(x + offset, RING), z, core), device_id_type=MESH
        )
    pl.semaphore_wait(barrier, 3)
    copies = []
    for offset in (1, 2, 3):
        peer = lax.rem(x + offset, RING)
        one = pltpu.make_async_remote_copy(
            src_ref=attended.at[peer], dst_ref=held.at[x], send_sem=send.at[offset - 1],
            recv_sem=recv.at[offset - 1], device_id=device(peer, z, core), device_id_type=MESH,
        )
        one.start()
        copies.append(one)
    held[x] = attended[x]
    for offset in (1, 2, 3):
        peer = lax.rem(x + 4 - offset, RING)
        pltpu.make_async_remote_copy(
            src_ref=attended.at[peer], dst_ref=held.at[peer], send_sem=send.at[offset - 1],
            recv_sem=recv.at[offset - 1], device_id=device(peer, z, core), device_id_type=MESH,
        ).wait_recv()
    summed = held[...].reshape(D, SEQ)
    numerator = lax.dot_general(summed, wo_all[...], TN, preferred_element_type=F32)
    out[0] = (numerator / total[0:1, 0:1]).astype(BF16)
    for one in copies:
        one.wait_send()


VMEM = pl.BlockSpec(memory_space=pltpu.VMEM)
SMEM = pl.BlockSpec(memory_space=pltpu.SMEM)


def shards(tokens, norm_gain, w_query, w_key, w_value, w_out, owner_map, pair_images, pair_count, confidence):
    kv, qt, weights, total, wo_all = pl.pallas_call(
        gather_kernel,
        out_shape=(
            jax.ShapeDtypeStruct((2 * PLANE, 2 * WIDE, SEQ), BF16),
            jax.ShapeDtypeStruct((RING, WIDE, SEQ), BF16),
            jax.ShapeDtypeStruct((8, 128), I32),
            jax.ShapeDtypeStruct((8, 128), F32),
            jax.ShapeDtypeStruct((D, D), BF16),
        ),
        in_specs=[VMEM] * 10,
        out_specs=(VMEM,) * 5,
        scratch_shapes=[
            pltpu.VMEM((PLANE, SEQ, D), BF16),
            pltpu.VMEM((RING, 32, 640), BF16),
            pltpu.VMEM((2, PLANE, 32, 640), BF16),
            pltpu.VMEM((2, PLANE, 32, D), BF16),
            pltpu.VMEM((2, PLANE, 8, 128), I32),
            pltpu.VMEM((640, D), BF16),
            pltpu.SemaphoreType.DMA((61,)),
            pltpu.SemaphoreType.DMA((61,)),
            pltpu.SemaphoreType.DMA((PLANE,)),
            pltpu.SemaphoreType.DMA((PLANE,)),
        ],
        compiler_params=pltpu.CompilerParams(
            collective_id=0, has_side_effects=True, vmem_limit_bytes=48 * 1024 * 1024
        ),
        name="gather_project",
    )(
        tokens, norm_gain.reshape(1, D), w_query, w_key, w_value, w_out,
        owner_map, pair_images, pair_count.reshape(1, 1), confidence,
    )
    attended = pl.pallas_call(
        attend_kernel,
        out_shape=jax.ShapeDtypeStruct((RING, WIDE, SEQ), BF16),
        in_specs=[SMEM, VMEM, VMEM],
        out_specs=VMEM,
        scratch_shapes=[
            pltpu.VMEM((RING, WIDE, 3 * SEQ), BF16),
            pltpu.VMEM((RING, 3, 64, 256), F32),
            pltpu.SMEM((136,), I32),
            pltpu.SMEM((136,), I32),
        ],
        compiler_params=pltpu.CompilerParams(vmem_limit_bytes=48 * 1024 * 1024),
        name="attend",
    )(weights, kv, qt)
    return pl.pallas_call(
        output_kernel,
        out_shape=jax.ShapeDtypeStruct((1, SEQ, D), BF16),
        in_specs=[VMEM] * 3,
        out_specs=VMEM,
        scratch_shapes=[
            pltpu.VMEM((RING, WIDE, SEQ), BF16),
            pltpu.SemaphoreType.DMA((3,)),
            pltpu.SemaphoreType.DMA((3,)),
        ],
        compiler_params=pltpu.CompilerParams(
            collective_id=1, has_side_effects=True, vmem_limit_bytes=48 * 1024 * 1024
        ),
        name="exchange_output",
    )(attended, wo_all, total)


def solution(mesh):
    both = P(("group", "shard"))
    in_specs = (
        P(("group", "shard"), None, None),
        P(),
        P("shard", None),
        P("shard", None),
        P("shard", None),
        P("shard", None),
        P("group", None),
        P(("group", "shard"), None),
        both,
        P(("group", "shard"), None),
    )
    out_specs = P(("group", "shard"), None, None)
    return jax.shard_map(shards, mesh=mesh, in_specs=in_specs, out_specs=out_specs, check_vma=False)
```

time: 839 us -> 89 us (0.11)
  the two profiles are of different devices: /device:TPU:1 before, /device:TPU:17 now
where the time goes in v1:
time: 89 us; the launch traced here: 88.5 us
  Pallas kernels  80.2 us (90%)
  local copies, waits for them, and re-layouts  7.6 us (9%)
    pallas_call x1, Pallas kernels, shards(): pl.pallas_call(gather_kernel, out_shape=(jax.ShapeDtypeStruct((2 * PLANE,...  54.4 us
    pallas_call x1, Pallas kernels, shards(): pl.pallas_call(attend_kernel, out_shape=jax.ShapeDtypeStruct((RING, WIDE,...  19.1 us
    unnamed x15, local copies, waits for them, and re-layouts  6.91 us
    pallas_call x1, Pallas kernels, shards(): pl.pallas_call(output_kernel, out_shape=jax.ShapeDtypeStruct((1, SEQ, D),...  6.63 us

profile of v1, /device:TPU:17, one launch (start us, length us, event | category | flops | bytes accessed | tf_op | source)
XLA Modules:
  0.0 88.5 jit_solution(12895355791362579386)
XLA Ops:
  0.7 0.7 reshape.6.gain
  1.3 0.8 copy.11.pimg
  2.1 0.8 copy.12.conf
  2.8 0.0 copy-start
  2.9 1.0 %copy-done = bf16[1,192,768]{2,1,0:T(8,128)(2,1)S(1)} copy-done((bf16[1,192,768]{2,1,0:T(8,128)(2,1)S(1)}, bf16[1,192,768]{2,1,0:T(8,128)(2,1)}, u32[]{:S(2)}) %copy-start) | copy-done | bytes 294936
  3.8 0.0 copy-start.1
  3.8 0.8 copy-done.1
  4.6 0.0 copy-start.2
  4.6 0.8 copy-done.2
  5.3 0.0 copy-start.3
  5.4 0.8 copy-done.3
  6.1 0.0 copy-start.4
  6.1 0.8 copy-done.4
  6.9 0.0 copy-start.5
  6.9 0.7 copy-done.5
  7.5 54.4 %gather_project.1 = (bf16[32,384,192]{2,1,0:T(8,128)(2,1)}, bf16[4,192,192]{2,1,0:T(8,128)(2,1)S(1)}, s32[8,128]{1,0:T(8,128)S(1)}, f32[8,128]{1,0:T(8,128)S(1)}, bf16[768,768]{1,0:T(8,128)(2,1)S(1)}) custom-call(bf16[1,192,768]{2,1,0:T(8,128)(2,1)S(1)} %copy-done, f32[1,768]{1,0:T(1,128)S(1)} %reshape.6.gain, bf16[24,768]{1,0:T(8,128)(2,1)S(1)} %copy-done.1, ...), custom_call_target="tpu_custom_call" | custom-call | tf_op jit(solution)/shard_map/gather_project/pallas_call | solution.py:373
  62.0 19.1 %attend.1.attended = bf16[4,192,192]{2,1,0:T(8,128)(2,1)S(1)} custom-call(s32[8,128]{1,0:T(8,128)S(1)} %get-tuple-element.10.weights, bf16[32,384,192]{2,1,0:T(8,128)(2,1)} %get-tuple-element.11.kv, bf16[4,192,192]{2,1,0:T(8,128)(2,1)S(1)} %get-tuple-element.12.qt), custom_call_target="tpu_custom_call" | custom-call | tf_op jit(solution)/shard_map/attend/pallas_call | solution.py:404
  81.1 6.6 %exchange_output.1 = bf16[1,192,768]{2,1,0:T(8,128)(2,1)S(1)} custom-call(bf16[4,192,192]{2,1,0:T(8,128)(2,1)S(1)} %attend.1.attended, bf16[768,768]{1,0:T(8,128)(2,1)S(1)} %get-tuple-element.13.wo_all, f32[8,128]{1,0:T(8,128)S(1)} %get-tuple-element.14.total), custom_call_target="tpu_custom_call" | custom-call | tf_op jit(solution)/shard_map/exchange_output/pallas_call | solution.py:418
  87.7 0.7 copy.15
Async XLA Ops:
  2.8 1.0 %copy-start = (bf16[1,192,768]{2,1,0:T(8,128)(2,1)S(1)}, bf16[1,192,768]{2,1,0:T(8,128)(2,1)}, u32[]{:S(2)}) copy-start(bf16[1,192,768]{2,1,0:T(8,128)(2,1)} %tok.1) | copy-start | bytes 884740
  3.8 0.8 copy-start.1
  4.6 0.8 copy-start.2
  5.3 0.8 copy-start.3
  6.1 0.8 copy-start.4
  6.9 0.7 copy-start.5

commit v2 on v1

v2 whole, which is shorter than its diff:
```python
import math

import jax
import jax.numpy as jnp
from jax import lax
from jax.experimental import pallas as pl
from jax.experimental.pallas import tpu as pltpu
from jax.sharding import PartitionSpec as P

MESH = pl.DeviceIdType.MESH
F32, BF16, I32 = jnp.float32, jnp.bfloat16, jnp.int32
SEQ, D, RING, PLANE = 192, 768, 4, 16
WIDE = 192
ROWS = 24
NT = (((1,), (1,)), ((), ()))
TN = (((0,), (0,)), ((), ()))
FIRST = (0, 3, 1, 2)


def place():
    shard = lax.axis_index("shard")
    core = lax.rem(shard, 2)
    chip = lax.div(shard, 2)
    return lax.rem(chip, RING), lax.div(chip, RING), core


def device(x, z, core):
    return {"shard": (z * RING + x) * 2 + core}


def gather_kernel(
    tok_h, gain_h, wq_h, wk_h, wv_h, wo_h, omap_h, pimg_h, pcnt_h, conf_h,
    kv, both, third, weights, total, wo_all,
    tok, gain, wq, wk, wv, wo, omap, pimg, pcnt, conf,
    img, staged, wplane, woplane, lists, wt, load, send, recv, pair_send, pair_recv,
):
    x, z, core = place()
    y = lax.axis_index("group")
    chip = z * RING + x

    def turn(value, offset):
        return lax.rem(value + offset, RING)

    def slot(ox, oz):
        return turn(z, oz) * RING + turn(x, ox)

    sibling = device(x, z, 1 - core)
    loads = [
        pltpu.make_async_copy(source, target, load.at[n])
        for n, (source, target) in enumerate((
            (tok_h, tok), (gain_h, gain), (wq_h, wq), (wk_h, wk), (wv_h, wv), (wo_h, wo),
            (omap_h, omap), (pimg_h, pimg), (pcnt_h, pcnt), (conf_h, conf),
        ))
    ]
    for one in loads:
        one.start()
    barrier = pltpu.get_barrier_semaphore()
    for offset in (1, 2, 3):
        for peer in (device(turn(x, offset), z, core), device(x, turn(z, offset), core), {"group": turn(y, offset)}):
            pl.semaphore_signal(barrier, 1, device_id=peer, device_id_type=MESH)
    pl.semaphore_signal(barrier, 1, device_id=sibling, device_id_type=MESH)

    for one in loads:
        one.wait()
    values = tok[0].astype(F32)
    centred = values - jnp.mean(values, axis=-1, keepdims=True)
    variance = jnp.mean(centred * centred, axis=-1, keepdims=True)
    img[chip] = (centred * lax.rsqrt(variance + 1e-05) * gain[...].reshape(1, D)).astype(BF16)

    square = (lax.broadcasted_iota(I32, (32, 32), 0), lax.broadcasted_iota(I32, (32, 32), 1))
    owners = jnp.sum(jnp.where(square[0] == square[1], omap[...], 0), axis=1, keepdims=True)
    image = lax.broadcasted_iota(I32, (32, 8), 0)
    stored = [
        jnp.sum(jnp.where(pimg[r:r + 1, :] == image, owners, 0), axis=0, keepdims=True) for r in (0, 1)
    ]
    listed = lax.broadcasted_iota(I32, (2, 8), 1) < pcnt[0]
    entries = jnp.concatenate(stored + [jnp.where(listed, conf[...], 0), jnp.zeros((4, 8), I32)], axis=0)
    entries = jnp.concatenate([entries, jnp.zeros((8, 120), I32)], axis=1)
    lists[core, chip] = pltpu.roll(entries, 8 * chip, 1)

    @pl.when(x == y)
    def _():
        parts = [w[...].astype(F32) for w in (wq, wk, wv)]
        for g in range(RING):
            cols = [w[:, g * WIDE:(g + 1) * WIDE] for w in parts] + [jnp.zeros((ROWS, 64), F32)]
            staged[g] = jnp.concatenate(cols, axis=1).astype(BF16)
        wplane[core, y, z] = staged[x]
        woplane[core, y, z] = wo[...]

    pl.semaphore_wait(barrier, 10)

    started = []

    def copy(source, target, number, where):
        return pltpu.make_async_remote_copy(
            src_ref=source, dst_ref=target, send_sem=send.at[number], recv_sem=recv.at[number],
            device_id=where, device_id_type=MESH,
        )

    def start(source, target, number, where):
        one = copy(source, target, number, where)
        one.start()
        started.append(one)

    def arrived(target, number):
        copy(target, target, number, sibling).wait_recv()

    def lists_x(base):
        for offset in (1, 2, 3):
            block = lists.at[core, chip]
            start(block, block, base + offset - 1, device(turn(x, offset), z, core))

    def lists_z(base):
        for offset in (1, 2, 3):
            arrived(lists.at[core, z * RING + turn(x, 4 - offset)], base + offset - 1)
        row = lists.at[core, pl.ds(z * RING, RING)]
        for offset in (1, 2, 3):
            start(row, row, base + 2 + offset, device(x, turn(z, offset), core))

    def lists_across(base):
        for offset in (1, 2, 3):
            arrived(lists.at[core, pl.ds(turn(z, 4 - offset) * RING, RING)], base + 2 + offset)
        start(lists.at[core], lists.at[core], base + 6, sibling)

    def rows_x(buffer, base, outgoing):
        block = buffer.at[core, y, z]

        @pl.when(x == y)
        def _():
            for offset in (1, 2, 3):
                source = outgoing.at[turn(x, offset)] if outgoing is staged else block
                copy(source, block, base + offset - 1, device(turn(x, offset), z, core)).start()

    def rows_x_sent(buffer, base):
        @pl.when(x == y)
        def _():
            for offset in (1, 2, 3):
                copy(buffer.at[core, y, z], buffer.at[core, y, z], base + offset - 1, sibling).wait_send()

    def rows_z(buffer, base):
        block = buffer.at[core, y, z]

        @pl.when(x != y)
        def _():
            arrived(block, base + turn(x, 4 - y) - 1)

        for offset in (1, 2, 3):
            start(block, block, base + 2 + offset, device(x, turn(z, offset), core))

    def rows_y(buffer, base):
        for offset in (1, 2, 3):
            arrived(buffer.at[core, y, turn(z, 4 - offset)], base + 2 + offset)
        for offset in (1, 2, 3):
            block = buffer.at[core, y]
            start(block, block, base + 5 + offset, {"group": turn(y, offset)})

    def rows_across(buffer, base):
        for offset in (1, 2, 3):
            arrived(buffer.at[core, turn(y, 4 - offset)], base + 5 + offset)
        start(buffer.at[core], buffer.at[core], base + 9, sibling)

    def ended(buffer, number):
        arrived(buffer.at[1 - core], number)

    def piece(half, first, second, part=None):
        low, count = (96 * half, 96) if part is None else (96 * half + 48 * part, 48)
        where = slot(first, second) if half == 0 else slot(second, first)
        return img.at[where, pl.ds(low, count)]

    def neighbour(axis, direction):
        step = 1 if direction == 0 else 3
        return device(turn(x, step), z, core) if axis == 0 else device(x, turn(z, step), core)

    def first_ring(half, direction):
        start(piece(half, 0, 0), piece(half, 0, 0), 20 * half + direction, neighbour(half, direction))

    def first_forward(half, direction):
        block = piece(half, (3, 1)[direction], 0, direction)
        start(block, block, 20 * half + 2 + direction, neighbour(half, direction))

    def second_ring(half, k):
        for direction in (0, 1):
            block = piece(half, FIRST[k], 0)
            start(block, block, 20 * half + 4 + 4 * k + direction, neighbour(1 - half, direction))

    def second_forward(half, k, direction):
        block = piece(half, FIRST[k], (3, 1)[direction], direction)
        start(block, block, 20 * half + 6 + 4 * k + direction, neighbour(1 - half, direction))

    def got_first(half, direction):
        arrived(piece(half, (3, 1)[direction], 0), 20 * half + direction)

    def got_first_forward(half, direction):
        arrived(piece(half, 2, 0, direction), 20 * half + 2 + direction)

    def got_second(half, k, direction):
        arrived(piece(half, FIRST[k], (3, 1)[direction]), 20 * half + 4 + 4 * k + direction)

    def got_second_forward(half, k, direction):
        arrived(piece(half, FIRST[k], 2, direction), 20 * half + 6 + 4 * k + direction)

    def pair_copy(where, row):
        return pltpu.make_async_remote_copy(
            src_ref=kv.at[row], dst_ref=kv.at[row], send_sem=pair_send.at[where],
            recv_sem=pair_recv.at[where], device_id=sibling, device_id_type=MESH,
        )

    def project(count, offsets):
        def one(i, carried):
            where = slot(*offsets(i))
            row = where * 2 + core
            normed = img[where]
            kv[row, 0:WIDE, :] = lax.dot_general(
                normed, wt[WIDE:2 * WIDE, :], NT, preferred_element_type=F32
            ).astype(BF16)
            kv[row, WIDE:2 * WIDE, :] = lax.dot_general(
                wt[2 * WIDE:3 * WIDE, :], normed, NT, preferred_element_type=F32
            ).astype(BF16)
            pair_copy(where, row).start()
            return carried

        lax.fori_loop(0, count, one, 0)

    W0, L0, O0 = 40, 50, 57
    rows_x(wplane, W0, staged)
    lists_x(L0)
    for half in (0, 1):
        for direction in (0, 1):
            first_ring(half, direction)
        second_ring(half, 0)
    rows_z(wplane, W0)
    lists_z(L0)
    rows_x(woplane, O0, woplane)

    rows_y(wplane, W0)
    for direction in (0, 1):
        for half in (0, 1):
            got_first(half, direction)
            first_forward(half, direction)
            second_ring(half, 1 + direction)
    for direction in (0, 1):
        for half in (0, 1):
            got_second(half, 0, direction)
            second_forward(half, 0, direction)
    rows_across(wplane, W0)
    lists_across(L0)
    rows_z(woplane, O0)
    ended(wplane, W0 + 9)
    ended(lists, L0 + 6)

    for j in (0, 1):
        blocks = []
        for one in range(8 * j, 8 * j + 8):
            for c in (0, 1):
                blocks.append(wplane[c, one % RING, one // RING].astype(F32))
        wt[:, 384 * j:384 * (j + 1)] = jnp.concatenate(blocks, axis=0).T.astype(BF16)
    project(1, lambda i: (i, i))
    project(4, lambda i: ((1 + 2 * (i % 2)) * (1 - i // 2), (1 + 2 * (i % 2)) * (i // 2)))

    tables = [jnp.sum(lists[c], axis=0) for c in (0, 1)]
    attended = lax.broadcasted_iota(I32, (32, 128), 0)

    def weight_column(querying):
        taken = jnp.zeros((32, 128), I32)
        for table in tables:
            for here, there in ((0, 1), (1, 0)):
                given = jnp.where(table[here:here + 1, :] == querying, table[2 + here:3 + here, :], 0)
                taken = taken + jnp.where(table[there:there + 1, :] == attended, given, 0)
        return jnp.sum(taken, axis=1, keepdims=True)

    column = lax.broadcasted_iota(I32, (32, 128), 1)
    by_query = jnp.zeros((32, 128), I32)
    for i in range(RING):
        by_query = jnp.where(column == i, weight_column((z * RING + i) * 2 + core), by_query)
    weights[...] = by_query
    own = jnp.sum(weight_column(chip * 2 + core).astype(F32), axis=0, keepdims=True)
    total[...] = jnp.broadcast_to(1.0 + own, (8, 128))

    for half in (0, 1):
        for direction in (0, 1):
            got_first_forward(half, direction)
        second_ring(half, 3)
    for k in (1, 2):
        for direction in (0, 1):
            for half in (0, 1):
                got_second(half, k, direction)
                second_forward(half, k, direction)
    for half in (0, 1):
        for direction in (0, 1):
            got_second_forward(half, 0, direction)
    rows_y(woplane, O0)
    project(4, lambda i: (1 + 2 * (i // 2), 1 + 2 * (i % 2)))
    project(2, lambda i: (2 * (1 - i), 2 * i))

    def one_query(i, carried):
        query = lax.dot_general(
            wt[0:WIDE, :], img[z * RING + i], NT, preferred_element_type=F32
        ).astype(BF16)
        both[i] = jnp.zeros((128, 2 * SEQ), BF16)
        for h in (0, 1):
            both[i, 64 * h:64 * (h + 1), SEQ * h:SEQ * (h + 1)] = query[64 * h:64 * (h + 1), :]
        third[i] = query[128:192, :]
        return carried

    lax.fori_loop(0, RING, one_query, 0)

    for direction in (0, 1):
        for half in (0, 1):
            got_second(half, 3, direction)
            second_forward(half, 3, direction)
    for k in (1, 2):
        for direction in (0, 1):
            for half in (0, 1):
                got_second_forward(half, k, direction)
    rows_across(woplane, O0)
    project(4, lambda i: (
        2 * (1 - i // 2) + (1 + 2 * (i % 2)) * (i // 2),
        (1 + 2 * (i % 2)) * (1 - i // 2) + 2 * (i // 2),
    ))
    ended(woplane, O0 + 9)
    for one in range(PLANE):
        blocks = [woplane[c, one % RING, one // RING].astype(F32) for c in (0, 1)]
        wo_all[2 * ROWS * one:2 * ROWS * (one + 1), :] = jnp.concatenate(blocks, axis=0).astype(BF16)
    for half in (0, 1):
        for direction in (0, 1):
            got_second_forward(half, 3, direction)
    project(1, lambda i: (i + 2, i + 2))
    for one in started:
        one.wait_send()
    rows_x_sent(wplane, W0)
    rows_x_sent(woplane, O0)

    def drain(where, carried):
        pair_copy(where, where * 2 + core).wait_send()
        pair_copy(where, where * 2 + 1 - core).wait_recv()
        return carried

    lax.fori_loop(0, PLANE, drain, 0)


WINDOWS = ((0, 256, 0), (128, 384, 64), (0, 192, 0))
TOGETHER = 6


def attend_kernel(weights, kv, both, third, out, acc, chosen, chosen_weight):
    acc[...] = jnp.zeros_like(acc)

    def note(number, count):
        weight = weights[number // RING, number % RING]
        chosen[count] = number
        chosen_weight[count] = weight
        return count + jnp.where(weight > 0, 1, 0)

    count = lax.fori_loop(0, 128, note, 0, unroll=8)
    for extra in range(TOGETHER - 1):
        chosen[count + extra] = 0
        chosen_weight[count + extra] = 0
    factor = math.log2(math.e) / 8.0

    def attention(scores):
        top = jnp.max(scores, axis=0, keepdims=True)
        expo = jnp.exp2((scores - top) * factor)
        return expo.astype(BF16), 1.0 / jnp.sum(expo, axis=0, keepdims=True)

    def several(step, carried):
        entries = [TOGETHER * step + part for part in range(TOGETHER)]
        places = [(chosen[entry] // RING, chosen[entry] % RING) for entry in entries]
        given = [chosen_weight[entry].astype(F32) for entry in entries]
        scores = [
            (
                jnp.dot(kv[t, 0:WIDE, 0:128], both[i], preferred_element_type=F32),
                jnp.dot(kv[t, 0:WIDE, 128:192], third[i], preferred_element_type=F32),
            )
            for t, i in places
        ]
        shares = [[attention(part) for part in one] for one in scores]
        found = []
        for (t, _), share, weight in zip(places, shares, given):
            for h, (low, high, _) in enumerate(WINDOWS):
                expo, scale = share[h // 2]
                one = jnp.dot(
                    kv[t, WIDE + 64 * h:WIDE + 64 * (h + 1), :], expo[:, low:high],
                    preferred_element_type=F32,
                )
                found.append((one * scale[:, low:high]).astype(BF16).astype(F32) * weight)
        for n, (_, i) in enumerate(places):
            for h in range(3):
                one = found[3 * n + h]
                acc[i, h, :, 0:one.shape[1]] += one
        return carried

    lax.fori_loop(0, (count + TOGETHER - 1) // TOGETHER, several, 0)
    for i in range(RING):
        heads = [acc[i, h][:, low:low + SEQ] for h, (_, _, low) in enumerate(WINDOWS)]
        summed = jnp.concatenate(heads, axis=0).astype(BF16)
        out[i, 0:WIDE, :] = summed[:, 0:128]
        out[i, WIDE:WIDE + 96, :] = jnp.concatenate([summed[0:96, 128:192], summed[96:192, 128:192]], axis=1)


def output_kernel(attended, wo_all, total, out, held, summed, send, recv):
    x, z, core = place()
    barrier = pltpu.get_barrier_semaphore()
    for offset in (1, 2, 3):
        pl.semaphore_signal(
            barrier, 1, device_id=device(lax.rem(x + offset, RING), z, core), device_id_type=MESH
        )
    pl.semaphore_wait(barrier, 3)
    copies = []
    for offset in (1, 2, 3):
        peer = lax.rem(x + offset, RING)
        one = pltpu.make_async_remote_copy(
            src_ref=attended.at[peer], dst_ref=held.at[x], send_sem=send.at[offset - 1],
            recv_sem=recv.at[offset - 1], device_id=device(peer, z, core), device_id_type=MESH,
        )
        one.start()
        copies.append(one)

    def unpack(peer, block):
        row = pl.multiple_of(peer * WIDE, WIDE)
        summed[pl.ds(row, WIDE), 0:128] = block[0:WIDE, :]
        summed[pl.ds(row, 96), 128:192] = block[WIDE:WIDE + 96, 0:64]
        summed[pl.ds(row + 96, 96), 128:192] = block[WIDE:WIDE + 96, 64:128]

    unpack(x, attended[x])
    for offset in (1, 2, 3):
        peer = lax.rem(x + 4 - offset, RING)
        pltpu.make_async_remote_copy(
            src_ref=attended.at[peer], dst_ref=held.at[peer], send_sem=send.at[offset - 1],
            recv_sem=recv.at[offset - 1], device_id=device(peer, z, core), device_id_type=MESH,
        ).wait_recv()
        unpack(peer, held[peer])
    numerator = lax.dot_general(summed[...], wo_all[...], TN, preferred_element_type=F32)
    out[0] = (numerator / total[0:1, 0:1]).astype(BF16)
    for one in copies:
        one.wait_send()


VMEM = pl.BlockSpec(memory_space=pltpu.VMEM)
SMEM = pl.BlockSpec(memory_space=pltpu.SMEM)
HBM = pl.BlockSpec(memory_space=pltpu.HBM)


def shards(tokens, norm_gain, w_query, w_key, w_value, w_out, owner_map, pair_images, pair_count, confidence):
    kv, both, third, weights, total, wo_all = pl.pallas_call(
        gather_kernel,
        out_shape=(
            jax.ShapeDtypeStruct((2 * PLANE, 2 * WIDE, SEQ), BF16),
            jax.ShapeDtypeStruct((RING, 128, 2 * SEQ), BF16),
            jax.ShapeDtypeStruct((RING, 64, SEQ), BF16),
            jax.ShapeDtypeStruct((32, 128), I32),
            jax.ShapeDtypeStruct((8, 128), F32),
            jax.ShapeDtypeStruct((D, D), BF16),
        ),
        in_specs=[HBM] * 10,
        out_specs=(VMEM,) * 6,
        scratch_shapes=[
            pltpu.VMEM((1, SEQ, D), BF16),
            pltpu.VMEM((D,), F32),
            pltpu.VMEM((ROWS, D), BF16),
            pltpu.VMEM((ROWS, D), BF16),
            pltpu.VMEM((ROWS, D), BF16),
            pltpu.VMEM((ROWS, D), BF16),
            pltpu.VMEM((1, 32), I32),
            pltpu.VMEM((2, 8), I32),
            pltpu.SMEM((1,), I32),
            pltpu.VMEM((2, 8), I32),
            pltpu.VMEM((PLANE, SEQ, D), BF16),
            pltpu.VMEM((RING, ROWS, 640), BF16),
            pltpu.VMEM((2, RING, RING, ROWS, 640), BF16),
            pltpu.VMEM((2, RING, RING, ROWS, D), BF16),
            pltpu.VMEM((2, PLANE, 8, 128), I32),
            pltpu.VMEM((640, D), BF16),
            pltpu.SemaphoreType.DMA((10,)),
            pltpu.SemaphoreType.DMA((67,)),
            pltpu.SemaphoreType.DMA((67,)),
            pltpu.SemaphoreType.DMA((PLANE,)),
            pltpu.SemaphoreType.DMA((PLANE,)),
        ],
        compiler_params=pltpu.CompilerParams(
            collective_id=0, has_side_effects=True, vmem_limit_bytes=32 * 1024 * 1024
        ),
        name="gather_project",
    )(
        *[
            pltpu.with_memory_space_constraint(one, pltpu.HBM)
            for one in (tokens, norm_gain, w_query, w_key, w_value, w_out, owner_map, pair_images.T)
        ],
        pair_count, pltpu.with_memory_space_constraint(confidence.T, pltpu.HBM),
    )
    attended = pl.pallas_call(
        attend_kernel,
        out_shape=jax.ShapeDtypeStruct((RING, WIDE + 96, 128), BF16),
        in_specs=[SMEM, VMEM, VMEM, VMEM],
        out_specs=VMEM,
        scratch_shapes=[
            pltpu.VMEM((RING, 3, 64, 256), F32),
            pltpu.SMEM((136,), I32),
            pltpu.SMEM((136,), I32),
        ],
        compiler_params=pltpu.CompilerParams(vmem_limit_bytes=32 * 1024 * 1024),
        name="attend",
    )(weights, kv, both, third)
    return pl.pallas_call(
        output_kernel,
        out_shape=jax.ShapeDtypeStruct((1, SEQ, D), BF16),
        in_specs=[VMEM] * 3,
        out_specs=VMEM,
        scratch_shapes=[
            pltpu.VMEM((RING, WIDE + 96, 128), BF16),
            pltpu.VMEM((D, SEQ), BF16),
            pltpu.SemaphoreType.DMA((3,)),
            pltpu.SemaphoreType.DMA((3,)),
        ],
        compiler_params=pltpu.CompilerParams(
            collective_id=1, has_side_effects=True, vmem_limit_bytes=32 * 1024 * 1024
        ),
        name="exchange_output",
    )(attended, wo_all, total)


def solution(mesh):
    both = P(("group", "shard"))
    in_specs = (
        P(("group", "shard"), None, None),
        P(),
        P("shard", None),
        P("shard", None),
        P("shard", None),
        P("shard", None),
        P("group", None),
        P(("group", "shard"), None),
        both,
        P(("group", "shard"), None),
    )
    out_specs = P(("group", "shard"), None, None)
    return jax.shard_map(shards, mesh=mesh, in_specs=in_specs, out_specs=out_specs, check_vma=False)
```

time: 89 us -> 60.5 us (0.68)
  the two profiles are of different devices: /device:TPU:17 before, /device:TPU:1 now
where the time goes in v2:
time: 60.5 us; the launch traced here: 60.4 us
  Pallas kernels  59 us (98%)
  local copies, waits for them, and re-layouts  0.72 us (1%)
  between operations  0.67 us (1%)
    pallas_call x1, Pallas kernels, shards(): pl.pallas_call(gather_kernel, out_shape=(jax.ShapeDtypeStruct((2 * PLANE,...  42.3 us
    pallas_call x1, Pallas kernels, shards(): pl.pallas_call(attend_kernel, out_shape=jax.ShapeDtypeStruct((RING, WIDE...  9.21 us
    pallas_call x1, Pallas kernels, shards(): pl.pallas_call(output_kernel, out_shape=jax.ShapeDtypeStruct((1, SEQ, D),...  7.52 us

profile of v2, /device:TPU:1, one launch (start us, length us, event | category | flops | bytes accessed | tf_op | source)
XLA Modules:
  0.0 60.4 jit_solution(17797159406501236016)
XLA Ops:
  0.7 42.3 %gather_project.1 = (bf16[32,384,192]{2,1,0:T(8,128)(2,1)S(1)}, bf16[4,128,384]{2,1,0:T(8,128)(2,1)S(1)}, bf16[4,64,192]{2,1,0:T(8,128)(2,1)S(1)}, s32[32,128]{1...) custom-call(bf16[1,192,768]{2,1,0:T(8,128)(2,1)} %tok_h.1, f32[768]{0:T(1024)} %gain_h.1, ...), custom_call_target="tpu_custom_call" | custom-call | tf_op jit(solution)/shard_map/gather_project/pallas_call | solution.py:444
  42.9 9.2 %attend.1.attended = bf16[4,288,128]{2,1,0:T(8,128)(2,1)S(1)} custom-call(s32[32,128]{1,0:T(8,128)S(1)} %get-tuple-element.11.weights, bf16[32,384,192]{2,1,0:T(8,128)(2,1)S(1)} %get-tuple-element.12.kv, bf16[4,128,384]{2,1,0:T(8,128)(2,1)S(1)} %get-tuple-element.13.both, bf16[4,64,192]{2,1,0:T(8,128)(2,1)S(1)} %get-tuple-element.14.third), custom_call_target="tpu_custom_call" | custom-call | tf_op jit(solution)/shard_map/attend/pallas_call | solution.py:490
  52.2 7.5 %exchange_output.1 = bf16[1,192,768]{2,1,0:T(8,128)(2,1)S(1)} custom-call(bf16[4,288,128]{2,1,0:T(8,128)(2,1)S(1)} %attend.1.attended, bf16[768,768]{1,0:T(8,128)(2,1)S(1)} %get-tuple-element.15.wo_all, f32[8,128]{1,0:T(8,128)S(1)} %get-tuple-element.16.total), custom_call_target="tpu_custom_call" | custom-call | tf_op jit(solution)/shard_map/exchange_output/pallas_call | solution.py:503
  59.7 0.7 %copy.13 = bf16[1,192,768]{2,1,0:T(8,128)(2,1)} copy(bf16[1,192,768]{2,1,0:T(8,128)(2,1)S(1)} %exchange_output.1) | data formatting | bytes 589824

commit v3 on v2

--- a/solution.py
+++ b/solution.py
@@ -32,7 +32,7 @@
     tok_h, gain_h, wq_h, wk_h, wv_h, wo_h, omap_h, pimg_h, pcnt_h, conf_h,
     kv, both, third, weights, total, wo_all,
     tok, gain, wq, wk, wv, wo, omap, pimg, pcnt, conf,
-    img, staged, wplane, woplane, lists, wt, load, send, recv, pair_send, pair_recv,
+    img, passed, taken, staged, wplane, woplane, lists, wt, load, send, recv, pair_send, pair_recv,
 ):
     x, z, core = place()
     y = lax.axis_index("group")
@@ -162,42 +162,29 @@
     def ended(buffer, number):
         arrived(buffer.at[1 - core], number)
 
-    def piece(half, first, second, part=None):
+    def piece(ring, offset, half, part=None):
         low, count = (96 * half, 96) if part is None else (96 * half + 48 * part, 48)
-        where = slot(first, second) if half == 0 else slot(second, first)
+        where = (slot(offset, 0), slot(0, offset), slot(offset, 2))[ring]
         return img.at[where, pl.ds(low, count)]
 
-    def neighbour(axis, direction):
-        step = 1 if direction == 0 else 3
-        return device(turn(x, step), z, core) if axis == 0 else device(x, turn(z, step), core)
-
-    def first_ring(half, direction):
-        start(piece(half, 0, 0), piece(half, 0, 0), 20 * half + direction, neighbour(half, direction))
-
-    def first_forward(half, direction):
-        block = piece(half, (3, 1)[direction], 0, direction)
-        start(block, block, 20 * half + 2 + direction, neighbour(half, direction))
-
-    def second_ring(half, k):
+    def ring_send(ring, offset, half, part, direction, number):
+        step = (1, 3)[direction]
+        peer = device(x, turn(z, step), core) if ring == 1 else device(turn(x, step), z, core)
+        block = piece(ring, offset, half, part)
+        start(block, block, 8 * ring + 4 * half + number + direction, peer)
+
+    def ring_start(ring, half):
         for direction in (0, 1):
-            block = piece(half, FIRST[k], 0)
-            start(block, block, 20 * half + 4 + 4 * k + direction, neighbour(1 - half, direction))
-
-    def second_forward(half, k, direction):
-        block = piece(half, FIRST[k], (3, 1)[direction], direction)
-        start(block, block, 20 * half + 6 + 4 * k + direction, neighbour(1 - half, direction))
-
-    def got_first(half, direction):
-        arrived(piece(half, (3, 1)[direction], 0), 20 * half + direction)
-
-    def got_first_forward(half, direction):
-        arrived(piece(half, 2, 0, direction), 20 * half + 2 + direction)
-
-    def got_second(half, k, direction):
-        arrived(piece(half, FIRST[k], (3, 1)[direction]), 20 * half + 4 + 4 * k + direction)
-
-    def got_second_forward(half, k, direction):
-        arrived(piece(half, FIRST[k], 2, direction), 20 * half + 6 + 4 * k + direction)
+            ring_send(ring, 0, half, None, direction, 0)
+
+    def ring_pass(ring, half):
+        for direction in (0, 1):
+            arrived(piece(ring, (3, 1)[direction], half), 8 * ring + 4 * half + direction)
+            ring_send(ring, (3, 1)[direction], half, direction, direction, 2)
+
+    def ring_end(ring, half):
+        for direction in (0, 1):
+            arrived(piece(ring, 2, half, direction), 8 * ring + 4 * half + 2 + direction)
 
     def pair_copy(where, row):
         return pltpu.make_async_remote_copy(
@@ -205,48 +192,70 @@
             recv_sem=pair_recv.at[where], device_id=sibling, device_id_type=MESH,
         )
 
+    def projected(where):
+        normed = img[where]
+        keys = lax.dot_general(normed, wt[WIDE:2 * WIDE, :], NT, preferred_element_type=F32)
+        values = lax.dot_general(wt[2 * WIDE:3 * WIDE, :], normed, NT, preferred_element_type=F32)
+        kv[where * 2 + core, 0:WIDE, :] = keys.astype(BF16)
+        kv[where * 2 + core, WIDE:2 * WIDE, :] = values.astype(BF16)
+        pair_copy(where, where * 2 + core).start()
+        return keys, values
+
     def project(count, offsets):
         def one(i, carried):
-            where = slot(*offsets(i))
+            projected(slot(*offsets(i)))
+            return carried
+
+        lax.fori_loop(0, count, one, 0)
+
+    def project_and_pass(k):
+        keys, values = projected(slot(FIRST[k], 0))
+        passed[k - 1, 0:WIDE, :] = keys[:, 0:128].astype(BF16)
+        passed[k - 1, WIDE:2 * WIDE, :] = values[:, 0:128].astype(BF16)
+        passed[k - 1, 2 * WIDE:3 * WIDE, :] = jnp.concatenate(
+            [keys[:, 128:WIDE], values[:, 128:WIDE]], axis=1
+        ).astype(BF16)
+        for direction in (0, 1):
+            start(
+                passed.at[k - 1], taken.at[direction, k - 1], 22 + 2 * k + direction,
+                device(x, turn(z, (1, 3)[direction]), core),
+            )
+
+    def take(k):
+        for direction in (0, 1):
+            block = taken.at[direction, k - 1]
+            arrived(block, 22 + 2 * k + direction)
+            where = slot(FIRST[k], (3, 1)[direction])
             row = where * 2 + core
-            normed = img[where]
-            kv[row, 0:WIDE, :] = lax.dot_general(
-                normed, wt[WIDE:2 * WIDE, :], NT, preferred_element_type=F32
-            ).astype(BF16)
-            kv[row, WIDE:2 * WIDE, :] = lax.dot_general(
-                wt[2 * WIDE:3 * WIDE, :], normed, NT, preferred_element_type=F32
-            ).astype(BF16)
+            kv[row, :, 0:128] = block[0:2 * WIDE, :]
+            rest = block[2 * WIDE:3 * WIDE, :].astype(F32)
+            kv[row, 0:WIDE, 128:WIDE] = rest[:, 0:64].astype(BF16)
+            kv[row, WIDE:2 * WIDE, 128:WIDE] = rest[:, 64:128].astype(BF16)
             pair_copy(where, row).start()
-            return carried
-
-        lax.fori_loop(0, count, one, 0)
-
-    W0, L0, O0 = 40, 50, 57
+
+    W0, L0, O0 = 30, 40, 47
     rows_x(wplane, W0, staged)
     lists_x(L0)
-    for half in (0, 1):
-        for direction in (0, 1):
-            first_ring(half, direction)
-        second_ring(half, 0)
+    ring_start(0, 0)
+    ring_start(1, 0)
+    ring_start(0, 1)
     rows_z(wplane, W0)
+    ring_start(1, 1)
+    rows_x(woplane, O0, woplane)
     lists_z(L0)
-    rows_x(woplane, O0, woplane)
-
+    ring_pass(0, 0)
+    ring_pass(1, 0)
     rows_y(wplane, W0)
-    for direction in (0, 1):
-        for half in (0, 1):
-            got_first(half, direction)
-            first_forward(half, direction)
-            second_ring(half, 1 + direction)
-    for direction in (0, 1):
-        for half in (0, 1):
-            got_second(half, 0, direction)
-            second_forward(half, 0, direction)
+    ring_pass(1, 1)
+    ring_pass(0, 1)
+    rows_z(woplane, O0)
+    ring_end(1, 0)
+    ring_start(2, 0)
     rows_across(wplane, W0)
+    ring_end(1, 1)
+    ring_start(2, 1)
     lists_across(L0)
-    rows_z(woplane, O0)
     ended(wplane, W0 + 9)
-    ended(lists, L0 + 6)
 
     for j in (0, 1):
         blocks = []
@@ -254,43 +263,14 @@
             for c in (0, 1):
                 blocks.append(wplane[c, one % RING, one // RING].astype(F32))
         wt[:, 384 * j:384 * (j + 1)] = jnp.concatenate(blocks, axis=0).T.astype(BF16)
-    project(1, lambda i: (i, i))
-    project(4, lambda i: ((1 + 2 * (i % 2)) * (1 - i // 2), (1 + 2 * (i % 2)) * (i // 2)))
-
-    tables = [jnp.sum(lists[c], axis=0) for c in (0, 1)]
-    attended = lax.broadcasted_iota(I32, (32, 128), 0)
-
-    def weight_column(querying):
-        taken = jnp.zeros((32, 128), I32)
-        for table in tables:
-            for here, there in ((0, 1), (1, 0)):
-                given = jnp.where(table[here:here + 1, :] == querying, table[2 + here:3 + here, :], 0)
-                taken = taken + jnp.where(table[there:there + 1, :] == attended, given, 0)
-        return jnp.sum(taken, axis=1, keepdims=True)
-
-    column = lax.broadcasted_iota(I32, (32, 128), 1)
-    by_query = jnp.zeros((32, 128), I32)
-    for i in range(RING):
-        by_query = jnp.where(column == i, weight_column((z * RING + i) * 2 + core), by_query)
-    weights[...] = by_query
-    own = jnp.sum(weight_column(chip * 2 + core).astype(F32), axis=0, keepdims=True)
-    total[...] = jnp.broadcast_to(1.0 + own, (8, 128))
-
-    for half in (0, 1):
-        for direction in (0, 1):
-            got_first_forward(half, direction)
-        second_ring(half, 3)
-    for k in (1, 2):
-        for direction in (0, 1):
-            for half in (0, 1):
-                got_second(half, k, direction)
-                second_forward(half, k, direction)
-    for half in (0, 1):
-        for direction in (0, 1):
-            got_second_forward(half, 0, direction)
+    project_and_pass(1)
+    project_and_pass(2)
+    ring_end(0, 0)
+    ring_end(0, 1)
+    project_and_pass(3)
     rows_y(woplane, O0)
-    project(4, lambda i: (1 + 2 * (i // 2), 1 + 2 * (i % 2)))
-    project(2, lambda i: (2 * (1 - i), 2 * i))
+    project(4, lambda i: (0, i))
+    ended(lists, L0 + 6)
 
     def one_query(i, carried):
         query = lax.dot_general(
@@ -304,27 +284,40 @@
 
     lax.fori_loop(0, RING, one_query, 0)
 
-    for direction in (0, 1):
-        for half in (0, 1):
-            got_second(half, 3, direction)
-            second_forward(half, 3, direction)
-    for k in (1, 2):
-        for direction in (0, 1):
-            for half in (0, 1):
-                got_second_forward(half, k, direction)
+    tables = [jnp.sum(lists[c], axis=0) for c in (0, 1)]
+    attended = lax.broadcasted_iota(I32, (32, 128), 0)
+
+    def weight_column(querying):
+        taken = jnp.zeros((32, 128), I32)
+        for table in tables:
+            for here, there in ((0, 1), (1, 0)):
+                given = jnp.where(table[here:here + 1, :] == querying, table[2 + here:3 + here, :], 0)
+                taken = taken + jnp.where(table[there:there + 1, :] == attended, given, 0)
+        return jnp.sum(taken, axis=1, keepdims=True)
+
+    column = lax.broadcasted_iota(I32, (32, 128), 1)
+    by_query = jnp.zeros((32, 128), I32)
+    for i in range(RING):
+        by_query = jnp.where(column == i, weight_column((z * RING + i) * 2 + core), by_query)
+    weights[...] = by_query
+    own = jnp.sum(weight_column(chip * 2 + core).astype(F32), axis=0, keepdims=True)
+    total[...] = jnp.broadcast_to(1.0 + own, (8, 128))
+
+    ring_pass(2, 0)
+    take(1)
+    ring_pass(2, 1)
+    project(2, lambda i: (1 + 2 * i, 2))
     rows_across(woplane, O0)
-    project(4, lambda i: (
-        2 * (1 - i // 2) + (1 + 2 * (i % 2)) * (i // 2),
-        (1 + 2 * (i % 2)) * (1 - i // 2) + 2 * (i // 2),
-    ))
+    take(2)
+    ring_end(2, 0)
+    ring_end(2, 1)
+    project(1, lambda i: (i + 2, i + 2))
     ended(woplane, O0 + 9)
     for one in range(PLANE):
         blocks = [woplane[c, one % RING, one // RING].astype(F32) for c in (0, 1)]
         wo_all[2 * ROWS * one:2 * ROWS * (one + 1), :] = jnp.concatenate(blocks, axis=0).astype(BF16)
-    for half in (0, 1):
-        for direction in (0, 1):
-            got_second_forward(half, 3, direction)
-    project(1, lambda i: (i + 2, i + 2))
+    take(3)
+
     for one in started:
         one.wait_send()
     rows_x_sent(wplane, W0)
@@ -465,14 +458,16 @@
             pltpu.SMEM((1,), I32),
             pltpu.VMEM((2, 8), I32),
             pltpu.VMEM((PLANE, SEQ, D), BF16),
+            pltpu.VMEM((3, 3 * WIDE, 128), BF16),
+            pltpu.VMEM((2, 3, 3 * WIDE, 128), BF16),
             pltpu.VMEM((RING, ROWS, 640), BF16),
             pltpu.VMEM((2, RING, RING, ROWS, 640), BF16),
             pltpu.VMEM((2, RING, RING, ROWS, D), BF16),
             pltpu.VMEM((2, PLANE, 8, 128), I32),
             pltpu.VMEM((640, D), BF16),
             pltpu.SemaphoreType.DMA((10,)),
-            pltpu.SemaphoreType.DMA((67,)),
-            pltpu.SemaphoreType.DMA((67,)),
+            pltpu.SemaphoreType.DMA((57,)),
+            pltpu.SemaphoreType.DMA((57,)),
             pltpu.SemaphoreType.DMA((PLANE,)),
             pltpu.SemaphoreType.DMA((PLANE,)),
         ],

time: 60.5 us -> 57 us (0.942)
  Pallas kernels: 59 us -> 55.4 us
    pallas_call x1, Pallas kernels: 42.3 us -> 38.7 us  [shards(): pl.pallas_call(gather_kernel, out_shape=(jax.ShapeDtypeStruct((2 * PLANE,...]
where the time goes in v3:
time: 57 us; the launch traced here: 56.8 us
  Pallas kernels  55.4 us (97%)
  local copies, waits for them, and re-layouts  0.72 us (1%)
  between operations  0.67 us (1%)
    pallas_call x1, Pallas kernels, shards(): pl.pallas_call(gather_kernel, out_shape=(jax.ShapeDtypeStruct((2 * PLANE,...  38.7 us
    pallas_call x1, Pallas kernels, shards(): pl.pallas_call(attend_kernel, out_shape=jax.ShapeDtypeStruct((RING, WIDE...  9.22 us
    pallas_call x1, Pallas kernels, shards(): pl.pallas_call(output_kernel, out_shape=jax.ShapeDtypeStruct((1, SEQ, D),...  7.57 us

profile of v3, /device:TPU:1, one launch (start us, length us, event | category | flops | bytes accessed | tf_op | source)
XLA Modules:
  0.0 56.8 jit_solution(17953282944872056921)
XLA Ops:
  0.7 38.7 %gather_project.1 = (bf16[32,384,192]{2,1,0:T(8,128)(2,1)S(1)}, bf16[4,128,384]{2,1,0:T(8,128)(2,1)S(1)}, bf16[4,64,192]{2,1,0:T(8,128)(2,1)S(1)}, s32[32,128]{1...) custom-call(bf16[1,192,768]{2,1,0:T(8,128)(2,1)} %tok_h.1, f32[768]{0:T(1024)} %gain_h.1, ...), custom_call_target="tpu_custom_call" | custom-call | tf_op jit(solution)/shard_map/gather_project/pallas_call | solution.py:437
  39.3 9.2 %attend.1.attended = bf16[4,288,128]{2,1,0:T(8,128)(2,1)S(1)} custom-call(s32[32,128]{1,0:T(8,128)S(1)} %get-tuple-element.11.weights, bf16[32,384,192]{2,1,0:T(8,128)(2,1)S(1)} %get-tuple-element.12.kv, bf16[4,128,384]{2,1,0:T(8,128)(2,1)S(1)} %get-tuple-element.13.both, bf16[4,64,192]{2,1,0:T(8,128)(2,1)S(1)} %get-tuple-element.14.third), custom_call_target="tpu_custom_call" | custom-call | tf_op jit(solution)/shard_map/attend/pallas_call | solution.py:485
  48.5 7.6 %exchange_output.1 = bf16[1,192,768]{2,1,0:T(8,128)(2,1)S(1)} custom-call(bf16[4,288,128]{2,1,0:T(8,128)(2,1)S(1)} %attend.1.attended, bf16[768,768]{1,0:T(8,128)(2,1)S(1)} %get-tuple-element.15.wo_all, f32[8,128]{1,0:T(8,128)S(1)} %get-tuple-element.16.total), custom_call_target="tpu_custom_call" | custom-call | tf_op jit(solution)/shard_map/exchange_output/pallas_call | solution.py:498
  56.1 0.7 %copy.13 = bf16[1,192,768]{2,1,0:T(8,128)(2,1)} copy(bf16[1,192,768]{2,1,0:T(8,128)(2,1)S(1)} %exchange_output.1) | data formatting | bytes 589824

commit v4 on v3

--- a/solution.py
+++ b/solution.py
@@ -28,11 +28,18 @@
     return {"shard": (z * RING + x) * 2 + core}
 
 
+def in_order(planes, j):
+    blocks = [
+        planes[c][one % RING, one // RING].astype(F32) for one in range(8 * j, 8 * j + 8) for c in (0, 1)
+    ]
+    return jnp.concatenate(blocks, axis=0)
+
+
 def gather_kernel(
-    tok_h, gain_h, wq_h, wk_h, wv_h, wo_h, omap_h, pimg_h, pcnt_h, conf_h,
-    kv, both, third, weights, total, wo_all,
-    tok, gain, wq, wk, wv, wo, omap, pimg, pcnt, conf,
-    img, passed, taken, staged, wplane, woplane, lists, wt, load, send, recv, pair_send, pair_recv,
+    tok_h, gain_h, wq_h, wk_h, wv_h, wo_h, omap_h, pimg_h, pcnt, conf_h,
+    kv, both, third, directions, total, woplane,
+    tok, gain, wq, wk, wv, wo, omap, pimg, conf,
+    img, passed, taken, staged, staged_query, wplane, qplane, lists, wt, load, send, recv, pair_send, pair_recv,
 ):
     x, z, core = place()
     y = lax.axis_index("group")
@@ -49,7 +56,7 @@
         pltpu.make_async_copy(source, target, load.at[n])
         for n, (source, target) in enumerate((
             (tok_h, tok), (gain_h, gain), (wq_h, wq), (wk_h, wk), (wv_h, wv), (wo_h, wo),
-            (omap_h, omap), (pimg_h, pimg), (pcnt_h, pcnt), (conf_h, conf),
+            (omap_h, omap), (pimg_h, pimg), (conf_h, conf),
         ))
     ]
     for one in loads:
@@ -73,18 +80,22 @@
     stored = [
         jnp.sum(jnp.where(pimg[r:r + 1, :] == image, owners, 0), axis=0, keepdims=True) for r in (0, 1)
     ]
-    listed = lax.broadcasted_iota(I32, (2, 8), 1) < pcnt[0]
+    listed = lax.broadcasted_iota(I32, (2, 8), 1) < pcnt[...]
     entries = jnp.concatenate(stored + [jnp.where(listed, conf[...], 0), jnp.zeros((4, 8), I32)], axis=0)
     entries = jnp.concatenate([entries, jnp.zeros((8, 120), I32)], axis=1)
     lists[core, chip] = pltpu.roll(entries, 8 * chip, 1)
 
     @pl.when(x == y)
     def _():
-        parts = [w[...].astype(F32) for w in (wq, wk, wv)]
+        keys, values, queries = [w[...].astype(F32) for w in (wk, wv, wq)]
         for g in range(RING):
-            cols = [w[:, g * WIDE:(g + 1) * WIDE] for w in parts] + [jnp.zeros((ROWS, 64), F32)]
-            staged[g] = jnp.concatenate(cols, axis=1).astype(BF16)
+            low, high = g * WIDE, (g + 1) * WIDE
+            staged[g] = jnp.concatenate([keys[:, low:high], values[:, low:high]], axis=1).astype(BF16)
+            staged_query[g] = jnp.concatenate(
+                [queries[:, low:high], jnp.zeros((ROWS, 64), F32)], axis=1
+            ).astype(BF16)
         wplane[core, y, z] = staged[x]
+        qplane[core, y, z] = staged_query[x]
         woplane[core, y, z] = wo[...]
 
     pl.semaphore_wait(barrier, 10)
@@ -128,7 +139,7 @@
         @pl.when(x == y)
         def _():
             for offset in (1, 2, 3):
-                source = outgoing.at[turn(x, offset)] if outgoing is staged else block
+                source = block if outgoing is None else outgoing.at[turn(x, offset)]
                 copy(source, block, base + offset - 1, device(turn(x, offset), z, core)).start()
 
     def rows_x_sent(buffer, base):
@@ -194,8 +205,8 @@
 
     def projected(where):
         normed = img[where]
-        keys = lax.dot_general(normed, wt[WIDE:2 * WIDE, :], NT, preferred_element_type=F32)
-        values = lax.dot_general(wt[2 * WIDE:3 * WIDE, :], normed, NT, preferred_element_type=F32)
+        keys = lax.dot_general(normed, wt[0:WIDE, :], NT, preferred_element_type=F32)
+        values = lax.dot_general(wt[WIDE:2 * WIDE, :], normed, NT, preferred_element_type=F32)
         kv[where * 2 + core, 0:WIDE, :] = keys.astype(BF16)
         kv[where * 2 + core, WIDE:2 * WIDE, :] = values.astype(BF16)
         pair_copy(where, where * 2 + core).start()
@@ -233,22 +244,25 @@
             kv[row, WIDE:2 * WIDE, 128:WIDE] = rest[:, 64:128].astype(BF16)
             pair_copy(where, row).start()
 
-    W0, L0, O0 = 30, 40, 47
+    W0, L0, O0, Q0 = 30, 40, 47, 57
     rows_x(wplane, W0, staged)
+    rows_x(qplane, Q0, staged_query)
     lists_x(L0)
     ring_start(0, 0)
     ring_start(1, 0)
     ring_start(0, 1)
+    rows_x(woplane, O0, None)
     rows_z(wplane, W0)
+    rows_z(qplane, Q0)
     ring_start(1, 1)
-    rows_x(woplane, O0, woplane)
     lists_z(L0)
     ring_pass(0, 0)
     ring_pass(1, 0)
     rows_y(wplane, W0)
     ring_pass(1, 1)
+    rows_z(woplane, O0)
     ring_pass(0, 1)
-    rows_z(woplane, O0)
+    rows_y(qplane, Q0)
     ring_end(1, 0)
     ring_start(2, 0)
     rows_across(wplane, W0)
@@ -258,23 +272,25 @@
     ended(wplane, W0 + 9)
 
     for j in (0, 1):
-        blocks = []
-        for one in range(8 * j, 8 * j + 8):
-            for c in (0, 1):
-                blocks.append(wplane[c, one % RING, one // RING].astype(F32))
-        wt[:, 384 * j:384 * (j + 1)] = jnp.concatenate(blocks, axis=0).T.astype(BF16)
+        wt[0:2 * WIDE, 384 * j:384 * (j + 1)] = in_order([wplane.at[0], wplane.at[1]], j).T.astype(BF16)
     project_and_pass(1)
     project_and_pass(2)
     ring_end(0, 0)
     ring_end(0, 1)
     project_and_pass(3)
+    rows_across(qplane, Q0)
+    project(4, lambda i: (0, i))
     rows_y(woplane, O0)
-    project(4, lambda i: (0, i))
     ended(lists, L0 + 6)
+
+    ring_pass(2, 0)
+    ended(qplane, Q0 + 9)
+    for j in (0, 1):
+        wt[2 * WIDE:2 * WIDE + 256, 384 * j:384 * (j + 1)] = in_order([qplane.at[0], qplane.at[1]], j).T.astype(BF16)
 
     def one_query(i, carried):
         query = lax.dot_general(
-            wt[0:WIDE, :], img[z * RING + i], NT, preferred_element_type=F32
+            wt[2 * WIDE:3 * WIDE, :], img[z * RING + i], NT, preferred_element_type=F32
         ).astype(BF16)
         both[i] = jnp.zeros((128, 2 * SEQ), BF16)
         for h in (0, 1):
@@ -283,7 +299,10 @@
         return carried
 
     lax.fori_loop(0, RING, one_query, 0)
-
+    take(1)
+    ring_pass(2, 1)
+    project(2, lambda i: (1 + 2 * i, 2))
+    take(2)
     tables = [jnp.sum(lists[c], axis=0) for c in (0, 1)]
     attended = lax.broadcasted_iota(I32, (32, 128), 0)
 
@@ -296,31 +315,39 @@
         return jnp.sum(taken, axis=1, keepdims=True)
 
     column = lax.broadcasted_iota(I32, (32, 128), 1)
-    by_query = jnp.zeros((32, 128), I32)
+    by_query = [weight_column((z * RING + i) * 2 + core) for i in range(RING)]
+    used = jnp.zeros((32, 128), F32)
     for i in range(RING):
-        by_query = jnp.where(column == i, weight_column((z * RING + i) * 2 + core), by_query)
-    weights[...] = by_query
+        used = jnp.where((column == i) & (by_query[i] > 0), 1.0, used)
+    above = jnp.where(square[1] < square[0], 1.0, 0.0)
+    before = jnp.dot(above.astype(BF16), used.astype(BF16), preferred_element_type=F32)
+    in_column = jnp.sum(used, axis=0, keepdims=True)
+    first = jnp.zeros((1, 1), F32)
+    numbers, amounts = jnp.zeros((32, 128), I32), jnp.zeros((32, 128), I32)
+    for i in range(RING):
+        rank = (before[:, i:i + 1] + first).astype(I32)
+        here = jnp.where(by_query[i] > 0, rank, -1) == column
+        numbers = numbers + jnp.where(here, attended * RING + i, 0)
+        amounts = amounts + jnp.where(here, by_query[i], 0)
+        first = first + in_column[:, i:i + 1]
+    directions[0:1, :] = jnp.sum(numbers, axis=0, keepdims=True)
+    directions[1:2, :] = jnp.sum(amounts, axis=0, keepdims=True)
+    directions[2:3, :] = jnp.broadcast_to(first.astype(I32), (1, 128))
+    directions[3:8, :] = jnp.zeros((5, 128), I32)
     own = jnp.sum(weight_column(chip * 2 + core).astype(F32), axis=0, keepdims=True)
     total[...] = jnp.broadcast_to(1.0 + own, (8, 128))
 
-    ring_pass(2, 0)
-    take(1)
-    ring_pass(2, 1)
-    project(2, lambda i: (1 + 2 * i, 2))
-    rows_across(woplane, O0)
-    take(2)
     ring_end(2, 0)
     ring_end(2, 1)
     project(1, lambda i: (i + 2, i + 2))
-    ended(woplane, O0 + 9)
-    for one in range(PLANE):
-        blocks = [woplane[c, one % RING, one // RING].astype(F32) for c in (0, 1)]
-        wo_all[2 * ROWS * one:2 * ROWS * (one + 1), :] = jnp.concatenate(blocks, axis=0).astype(BF16)
     take(3)
 
+    for offset in (1, 2, 3):
+        arrived(woplane.at[core, turn(y, 4 - offset)], O0 + 5 + offset)
     for one in started:
         one.wait_send()
     rows_x_sent(wplane, W0)
+    rows_x_sent(qplane, Q0)
     rows_x_sent(woplane, O0)
 
     def drain(where, carried):
@@ -335,19 +362,9 @@
 TOGETHER = 6
 
 
-def attend_kernel(weights, kv, both, third, out, acc, chosen, chosen_weight):
+def attend_kernel(directions, kv, both, third, out, acc):
     acc[...] = jnp.zeros_like(acc)
-
-    def note(number, count):
-        weight = weights[number // RING, number % RING]
-        chosen[count] = number
-        chosen_weight[count] = weight
-        return count + jnp.where(weight > 0, 1, 0)
-
-    count = lax.fori_loop(0, 128, note, 0, unroll=8)
-    for extra in range(TOGETHER - 1):
-        chosen[count + extra] = 0
-        chosen_weight[count + extra] = 0
+    count = directions[2, 0]
     factor = math.log2(math.e) / 8.0
 
     def attention(scores):
@@ -357,8 +374,8 @@
 
     def several(step, carried):
         entries = [TOGETHER * step + part for part in range(TOGETHER)]
-        places = [(chosen[entry] // RING, chosen[entry] % RING) for entry in entries]
-        given = [chosen_weight[entry].astype(F32) for entry in entries]
+        places = [(directions[0, entry] // RING, directions[0, entry] % RING) for entry in entries]
+        given = [directions[1, entry].astype(F32) for entry in entries]
         scores = [
             (
                 jnp.dot(kv[t, 0:WIDE, 0:128], both[i], preferred_element_type=F32),
@@ -390,14 +407,16 @@
         out[i, WIDE:WIDE + 96, :] = jnp.concatenate([summed[0:96, 128:192], summed[96:192, 128:192]], axis=1)
 
 
-def output_kernel(attended, wo_all, total, out, held, summed, send, recv):
+def output_kernel(attended, woplane, total, out, wo_all, wo_both, held, send, recv):
     x, z, core = place()
+    sibling = device(x, z, 1 - core)
     barrier = pltpu.get_barrier_semaphore()
     for offset in (1, 2, 3):
         pl.semaphore_signal(
             barrier, 1, device_id=device(lax.rem(x + offset, RING), z, core), device_id_type=MESH
         )
-    pl.semaphore_wait(barrier, 3)
+    pl.semaphore_signal(barrier, 1, device_id=sibling, device_id_type=MESH)
+    pl.semaphore_wait(barrier, 4)
     copies = []
     for offset in (1, 2, 3):
         peer = lax.rem(x + offset, RING)
@@ -408,21 +427,35 @@
         one.start()
         copies.append(one)
 
-    def unpack(peer, block):
-        row = pl.multiple_of(peer * WIDE, WIDE)
-        summed[pl.ds(row, WIDE), 0:128] = block[0:WIDE, :]
-        summed[pl.ds(row, 96), 128:192] = block[WIDE:WIDE + 96, 0:64]
-        summed[pl.ds(row + 96, 96), 128:192] = block[WIDE:WIDE + 96, 64:128]
-
-    unpack(x, attended[x])
+    across = pltpu.make_async_remote_copy(
+        src_ref=woplane.at[core], dst_ref=wo_both.at[core], send_sem=send.at[3], recv_sem=recv.at[3],
+        device_id=sibling, device_id_type=MESH,
+    )
+    across.start()
+    copies.append(across)
+    wo_both[core] = woplane[core]
+    pltpu.make_async_remote_copy(
+        src_ref=woplane.at[core], dst_ref=wo_both.at[1 - core], send_sem=send.at[3], recv_sem=recv.at[3],
+        device_id=sibling, device_id_type=MESH,
+    ).wait_recv()
+    for j in (0, 1):
+        wo_all[384 * j:384 * (j + 1), :] = in_order([wo_both.at[0], wo_both.at[1]], j).astype(BF16)
+
+    def product(peer, block):
+        summed = jnp.concatenate(
+            [block[0:WIDE, :], jnp.concatenate([block[WIDE:, 0:64], block[WIDE:, 64:128]], axis=0)], axis=1
+        )
+        rows = pl.ds(pl.multiple_of(peer * WIDE, WIDE), WIDE)
+        return lax.dot_general(summed, wo_all[rows, :], TN, preferred_element_type=F32)
+
+    numerator = product(x, attended[x])
     for offset in (1, 2, 3):
         peer = lax.rem(x + 4 - offset, RING)
         pltpu.make_async_remote_copy(
             src_ref=attended.at[peer], dst_ref=held.at[peer], send_sem=send.at[offset - 1],
             recv_sem=recv.at[offset - 1], device_id=device(peer, z, core), device_id_type=MESH,
         ).wait_recv()
-        unpack(peer, held[peer])
-    numerator = lax.dot_general(summed[...], wo_all[...], TN, preferred_element_type=F32)
+        numerator += product(peer, held[peer])
     out[0] = (numerator / total[0:1, 0:1]).astype(BF16)
     for one in copies:
         one.wait_send()
@@ -434,17 +467,17 @@
 
 
 def shards(tokens, norm_gain, w_query, w_key, w_value, w_out, owner_map, pair_images, pair_count, confidence):
-    kv, both, third, weights, total, wo_all = pl.pallas_call(
+    kv, both, third, directions, total, woplane = pl.pallas_call(
         gather_kernel,
         out_shape=(
             jax.ShapeDtypeStruct((2 * PLANE, 2 * WIDE, SEQ), BF16),
             jax.ShapeDtypeStruct((RING, 128, 2 * SEQ), BF16),
             jax.ShapeDtypeStruct((RING, 64, SEQ), BF16),
-            jax.ShapeDtypeStruct((32, 128), I32),
+            jax.ShapeDtypeStruct((8, 128), I32),
             jax.ShapeDtypeStruct((8, 128), F32),
-            jax.ShapeDtypeStruct((D, D), BF16),
+            jax.ShapeDtypeStruct((2, RING, RING, ROWS, D), BF16),
         ),
-        in_specs=[HBM] * 10,
+        in_specs=[HBM] * 8 + [VMEM, HBM],
         out_specs=(VMEM,) * 6,
         scratch_shapes=[
             pltpu.VMEM((1, SEQ, D), BF16),
@@ -455,19 +488,19 @@
             pltpu.VMEM((ROWS, D), BF16),
             pltpu.VMEM((1, 32), I32),
             pltpu.VMEM((2, 8), I32),
-            pltpu.SMEM((1,), I32),
             pltpu.VMEM((2, 8), I32),
             pltpu.VMEM((PLANE, SEQ, D), BF16),
             pltpu.VMEM((3, 3 * WIDE, 128), BF16),
             pltpu.VMEM((2, 3, 3 * WIDE, 128), BF16),
-            pltpu.VMEM((RING, ROWS, 640), BF16),
-            pltpu.VMEM((2, RING, RING, ROWS, 640), BF16),
-            pltpu.VMEM((2, RING, RING, ROWS, D), BF16),
+            pltpu.VMEM((RING, ROWS, 2 * WIDE), BF16),
+            pltpu.VMEM((RING, ROWS, 256), BF16),
+            pltpu.VMEM((2, RING, RING, ROWS, 2 * WIDE), BF16),
+            pltpu.VMEM((2, RING, RING, ROWS, 256), BF16),
             pltpu.VMEM((2, PLANE, 8, 128), I32),
             pltpu.VMEM((640, D), BF16),
-            pltpu.SemaphoreType.DMA((10,)),
-            pltpu.SemaphoreType.DMA((57,)),
-            pltpu.SemaphoreType.DMA((57,)),
+            pltpu.SemaphoreType.DMA((9,)),
+            pltpu.SemaphoreType.DMA((67,)),
+            pltpu.SemaphoreType.DMA((67,)),
             pltpu.SemaphoreType.DMA((PLANE,)),
             pltpu.SemaphoreType.DMA((PLANE,)),
         ],
@@ -480,7 +513,7 @@
             pltpu.with_memory_space_constraint(one, pltpu.HBM)
             for one in (tokens, norm_gain, w_query, w_key, w_value, w_out, owner_map, pair_images.T)
         ],
-        pair_count, pltpu.with_memory_space_constraint(confidence.T, pltpu.HBM),
+        pair_count.reshape(1, 1), pltpu.with_memory_space_constraint(confidence.T, pltpu.HBM),
     )
     attended = pl.pallas_call(
         attend_kernel,
@@ -489,28 +522,27 @@
         out_specs=VMEM,
         scratch_shapes=[
             pltpu.VMEM((RING, 3, 64, 256), F32),
-            pltpu.SMEM((136,), I32),
-            pltpu.SMEM((136,), I32),
         ],
         compiler_params=pltpu.CompilerParams(vmem_limit_bytes=32 * 1024 * 1024),
         name="attend",
-    )(weights, kv, both, third)
+    )(directions, kv, both, third)
     return pl.pallas_call(
         output_kernel,
         out_shape=jax.ShapeDtypeStruct((1, SEQ, D), BF16),
         in_specs=[VMEM] * 3,
         out_specs=VMEM,
         scratch_shapes=[
+            pltpu.VMEM((D, D), BF16),
+            pltpu.VMEM((2, RING, RING, ROWS, D), BF16),
             pltpu.VMEM((RING, WIDE + 96, 128), BF16),
-            pltpu.VMEM((D, SEQ), BF16),
-            pltpu.SemaphoreType.DMA((3,)),
-            pltpu.SemaphoreType.DMA((3,)),
+            pltpu.SemaphoreType.DMA((4,)),
+            pltpu.SemaphoreType.DMA((4,)),
         ],
         compiler_params=pltpu.CompilerParams(
             collective_id=1, has_side_effects=True, vmem_limit_bytes=32 * 1024 * 1024
         ),
         name="exchange_output",
-    )(attended, wo_all, total)
+    )(attended, woplane, total)
 
 
 def solution(mesh):

time: 57 us -> 53.6 us (0.940)
  Pallas kernels: 55.4 us -> 52.1 us
    pallas_call x1, Pallas kernels: 9.22 us -> 6.62 us  [shards(): pl.pallas_call(attend_kernel, out_shape=jax.ShapeDtypeStruct((RING, WIDE...]
where the time goes in v4:
time: 53.6 us; the launch traced here: 53.5 us
  Pallas kernels  52.1 us (97%)
  local copies, waits for them, and re-layouts  0.72 us (1%)
  between operations  0.67 us (1%)
    pallas_call x1, Pallas kernels, shards(): pl.pallas_call(gather_kernel, out_shape=(jax.ShapeDtypeStruct((2 * PLANE,...  38.2 us
    pallas_call x1, Pallas kernels, shards(): pl.pallas_call(output_kernel, out_shape=jax.ShapeDtypeStruct((1, SEQ, D),...  7.22 us
    pallas_call x1, Pallas kernels, shards(): pl.pallas_call(attend_kernel, out_shape=jax.ShapeDtypeStruct((RING, WIDE...  6.62 us

profile of v4, /device:TPU:1, one launch (start us, length us, event | category | flops | bytes accessed | tf_op | source)
XLA Modules:
  0.0 53.5 jit_solution(3142915152744537063)
XLA Ops:
  0.7 38.2 %gather_project.1 = (bf16[32,384,192]{2,1,0:T(8,128)(2,1)S(1)}, bf16[4,128,384]{2,1,0:T(8,128)(2,1)S(1)}, bf16[4,64,192]{2,1,0:T(8,128)(2,1)S(1)}, s32[8,128]{1,...) custom-call(bf16[1,192,768]{2,1,0:T(8,128)(2,1)} %tok_h.1, f32[768]{0:T(1024)} %gain_h.1, ...), custom_call_target="tpu_custom_call" | custom-call | tf_op jit(solution)/shard_map/gather_project/pallas_call | solution.py:470
  38.9 6.6 %attend.1.attended = bf16[4,288,128]{2,1,0:T(8,128)(2,1)S(1)} custom-call(s32[8,128]{1,0:T(8,128)S(1)} %get-tuple-element.11.directions, bf16[32,384,192]{2,1,0:T(8,128)(2,1)S(1)} %get-tuple-element.12.kv, bf16[4,128,384]{2,1,0:T(8,128)(2,1)S(1)} %get-tuple-element.13.both, bf16[4,64,192]{2,1,0:T(8,128)(2,1)S(1)} %get-tuple-element.14.third), custom_call_target="tpu_custom_call" | custom-call | tf_op jit(solution)/shard_map/attend/pallas_call | solution.py:518
  45.5 7.2 %exchange_output.1 = bf16[1,192,768]{2,1,0:T(8,128)(2,1)S(1)} custom-call(bf16[4,288,128]{2,1,0:T(8,128)(2,1)S(1)} %attend.1.attended, bf16[2,4,4,24,768]{4,3,2,1,0:T(8,128)(2,1)S(1)} %get-tuple-element.15.woplane, f32[8,128]{1,0:T(8,128)S(1)} %get-tuple-element.16.total), custom_call_target="tpu_custom_call" | custom-call | tf_op jit(solution)/shard_map/exchange_output/pallas_call | solution.py:529
  52.8 0.7 %copy.13 = bf16[1,192,768]{2,1,0:T(8,128)(2,1)} copy(bf16[1,192,768]{2,1,0:T(8,128)(2,1)S(1)} %exchange_output.1) | data formatting | bytes 589824

commit v5 on v4

--- a/solution.py
+++ b/solution.py
@@ -28,9 +28,10 @@
     return {"shard": (z * RING + x) * 2 + core}
 
 
-def in_order(planes, j):
+def in_order(planes, j, turned=False):
     blocks = [
-        planes[c][one % RING, one // RING].astype(F32) for one in range(8 * j, 8 * j + 8) for c in (0, 1)
+        (planes[c][one // RING, one % RING] if turned else planes[c][one % RING, one // RING]).astype(F32)
+        for one in range(8 * j, 8 * j + 8) for c in (0, 1)
     ]
     return jnp.concatenate(blocks, axis=0)
 
@@ -96,7 +97,10 @@
             ).astype(BF16)
         wplane[core, y, z] = staged[x]
         qplane[core, y, z] = staged_query[x]
-        woplane[core, y, z] = wo[...]
+
+    @pl.when(z == y)
+    def _():
+        woplane[core, y, x] = wo[...]
 
     pl.semaphore_wait(barrier, 10)
 
@@ -133,34 +137,42 @@
             arrived(lists.at[core, pl.ds(turn(z, 4 - offset) * RING, RING)], base + 2 + offset)
         start(lists.at[core], lists.at[core], base + 6, sibling)
 
-    def rows_x(buffer, base, outgoing):
-        block = buffer.at[core, y, z]
-
-        @pl.when(x == y)
+    def along(axis, offset):
+        return device(turn(x, offset), z, core) if axis == 0 else device(x, turn(z, offset), core)
+
+    def rows_first(buffer, base, outgoing, axis):
+        here, there = (x, z) if axis == 0 else (z, x)
+        block = buffer.at[core, y, there]
+
+        @pl.when(here == y)
         def _():
             for offset in (1, 2, 3):
-                source = block if outgoing is None else outgoing.at[turn(x, offset)]
-                copy(source, block, base + offset - 1, device(turn(x, offset), z, core)).start()
-
-    def rows_x_sent(buffer, base):
-        @pl.when(x == y)
+                source = block if outgoing is None else outgoing.at[turn(here, offset)]
+                copy(source, block, base + offset - 1, along(axis, offset)).start()
+
+    def rows_first_sent(buffer, base, axis):
+        here, there = (x, z) if axis == 0 else (z, x)
+
+        @pl.when(here == y)
         def _():
             for offset in (1, 2, 3):
-                copy(buffer.at[core, y, z], buffer.at[core, y, z], base + offset - 1, sibling).wait_send()
-
-    def rows_z(buffer, base):
-        block = buffer.at[core, y, z]
-
-        @pl.when(x != y)
+                copy(buffer.at[core, y, there], buffer.at[core, y, there], base + offset - 1, sibling).wait_send()
+
+    def rows_second(buffer, base, axis):
+        here, there = (x, z) if axis == 0 else (z, x)
+        block = buffer.at[core, y, there]
+
+        @pl.when(here != y)
         def _():
-            arrived(block, base + turn(x, 4 - y) - 1)
-
-        for offset in (1, 2, 3):
-            start(block, block, base + 2 + offset, device(x, turn(z, offset), core))
-
-    def rows_y(buffer, base):
-        for offset in (1, 2, 3):
-            arrived(buffer.at[core, y, turn(z, 4 - offset)], base + 2 + offset)
+            arrived(block, base + turn(here, 4 - y) - 1)
+
+        for offset in (1, 2, 3):
+            start(block, block, base + 2 + offset, along(1 - axis, offset))
+
+    def rows_y(buffer, base, axis):
+        there = z if axis == 0 else x
+        for offset in (1, 2, 3):
+            arrived(buffer.at[core, y, turn(there, 4 - offset)], base + 2 + offset)
         for offset in (1, 2, 3):
             block = buffer.at[core, y]
             start(block, block, base + 5 + offset, {"group": turn(y, offset)})
@@ -221,20 +233,29 @@
 
     def project_and_pass(k):
         keys, values = projected(slot(FIRST[k], 0))
-        passed[k - 1, 0:WIDE, :] = keys[:, 0:128].astype(BF16)
-        passed[k - 1, WIDE:2 * WIDE, :] = values[:, 0:128].astype(BF16)
-        passed[k - 1, 2 * WIDE:3 * WIDE, :] = jnp.concatenate(
+        passed[k - 2, 0:WIDE, :] = keys[:, 0:128].astype(BF16)
+        passed[k - 2, WIDE:2 * WIDE, :] = values[:, 0:128].astype(BF16)
+        passed[k - 2, 2 * WIDE:3 * WIDE, :] = jnp.concatenate(
             [keys[:, 128:WIDE], values[:, 128:WIDE]], axis=1
         ).astype(BF16)
         for direction in (0, 1):
             start(
-                passed.at[k - 1], taken.at[direction, k - 1], 22 + 2 * k + direction,
+                passed.at[k - 2], taken.at[direction, k - 2], 22 + 2 * k + direction,
                 device(x, turn(z, (1, 3)[direction]), core),
             )
 
+    def tokens_pass(k):
+        block = img.at[slot(FIRST[k], 0)]
+        for direction in (0, 1):
+            start(block, block, 22 + 2 * k + direction, device(x, turn(z, (1, 3)[direction]), core))
+
+    def tokens_end(k):
+        for direction in (0, 1):
+            arrived(img.at[slot(FIRST[k], (3, 1)[direction])], 22 + 2 * k + direction)
+
     def take(k):
         for direction in (0, 1):
-            block = taken.at[direction, k - 1]
+            block = taken.at[direction, k - 2]
             arrived(block, 22 + 2 * k + direction)
             where = slot(FIRST[k], (3, 1)[direction])
             row = where * 2 + core
@@ -245,64 +266,34 @@
             pair_copy(where, row).start()
 
     W0, L0, O0, Q0 = 30, 40, 47, 57
-    rows_x(wplane, W0, staged)
-    rows_x(qplane, Q0, staged_query)
+    rows_first(wplane, W0, staged, 0)
+    rows_first(qplane, Q0, staged_query, 0)
     lists_x(L0)
     ring_start(0, 0)
     ring_start(1, 0)
     ring_start(0, 1)
-    rows_x(woplane, O0, None)
-    rows_z(wplane, W0)
-    rows_z(qplane, Q0)
+    rows_first(woplane, O0, None, 1)
+    rows_second(wplane, W0, 0)
+    rows_second(qplane, Q0, 0)
     ring_start(1, 1)
     lists_z(L0)
     ring_pass(0, 0)
     ring_pass(1, 0)
-    rows_y(wplane, W0)
+    rows_second(woplane, O0, 1)
+    rows_y(wplane, W0, 0)
     ring_pass(1, 1)
-    rows_z(woplane, O0)
     ring_pass(0, 1)
-    rows_y(qplane, Q0)
+    tokens_pass(1)
+    rows_y(qplane, Q0, 0)
     ring_end(1, 0)
     ring_start(2, 0)
     rows_across(wplane, W0)
     ring_end(1, 1)
     ring_start(2, 1)
     lists_across(L0)
-    ended(wplane, W0 + 9)
-
-    for j in (0, 1):
-        wt[0:2 * WIDE, 384 * j:384 * (j + 1)] = in_order([wplane.at[0], wplane.at[1]], j).T.astype(BF16)
-    project_and_pass(1)
-    project_and_pass(2)
-    ring_end(0, 0)
-    ring_end(0, 1)
-    project_and_pass(3)
-    rows_across(qplane, Q0)
-    project(4, lambda i: (0, i))
-    rows_y(woplane, O0)
+    rows_y(woplane, O0, 1)
     ended(lists, L0 + 6)
 
-    ring_pass(2, 0)
-    ended(qplane, Q0 + 9)
-    for j in (0, 1):
-        wt[2 * WIDE:2 * WIDE + 256, 384 * j:384 * (j + 1)] = in_order([qplane.at[0], qplane.at[1]], j).T.astype(BF16)
-
-    def one_query(i, carried):
-        query = lax.dot_general(
-            wt[2 * WIDE:3 * WIDE, :], img[z * RING + i], NT, preferred_element_type=F32
-        ).astype(BF16)
-        both[i] = jnp.zeros((128, 2 * SEQ), BF16)
-        for h in (0, 1):
-            both[i, 64 * h:64 * (h + 1), SEQ * h:SEQ * (h + 1)] = query[64 * h:64 * (h + 1), :]
-        third[i] = query[128:192, :]
-        return carried
-
-    lax.fori_loop(0, RING, one_query, 0)
-    take(1)
-    ring_pass(2, 1)
-    project(2, lambda i: (1 + 2 * i, 2))
-    take(2)
     tables = [jnp.sum(lists[c], axis=0) for c in (0, 1)]
     attended = lax.broadcasted_iota(I32, (32, 128), 0)
 
@@ -337,6 +328,39 @@
     own = jnp.sum(weight_column(chip * 2 + core).astype(F32), axis=0, keepdims=True)
     total[...] = jnp.broadcast_to(1.0 + own, (8, 128))
 
+    ended(wplane, W0 + 9)
+
+    for j in (0, 1):
+        wt[0:2 * WIDE, 384 * j:384 * (j + 1)] = in_order([wplane.at[0], wplane.at[1]], j).T.astype(BF16)
+    project_and_pass(2)
+    ring_end(0, 0)
+    ring_end(0, 1)
+    project_and_pass(3)
+    rows_across(qplane, Q0)
+    project(4, lambda i: (0, i))
+    project(1, lambda i: (i + 3, i))
+
+    ring_pass(2, 0)
+    ended(qplane, Q0 + 9)
+    for j in (0, 1):
+        wt[2 * WIDE:2 * WIDE + 256, 384 * j:384 * (j + 1)] = in_order([qplane.at[0], qplane.at[1]], j).T.astype(BF16)
+
+    def one_query(i, carried):
+        query = lax.dot_general(
+            wt[2 * WIDE:3 * WIDE, :], img[z * RING + i], NT, preferred_element_type=F32
+        ).astype(BF16)
+        both[i] = jnp.zeros((128, 2 * SEQ), BF16)
+        for h in (0, 1):
+            both[i, 64 * h:64 * (h + 1), SEQ * h:SEQ * (h + 1)] = query[64 * h:64 * (h + 1), :]
+        third[i] = query[128:192, :]
+        return carried
+
+    lax.fori_loop(0, RING, one_query, 0)
+    tokens_end(1)
+    project(2, lambda i: (i * 0 + 3, 1 + 2 * i))
+    ring_pass(2, 1)
+    project(2, lambda i: (1 + 2 * i, 2))
+    take(2)
     ring_end(2, 0)
     ring_end(2, 1)
     project(1, lambda i: (i + 2, i + 2))
@@ -346,9 +370,9 @@
         arrived(woplane.at[core, turn(y, 4 - offset)], O0 + 5 + offset)
     for one in started:
         one.wait_send()
-    rows_x_sent(wplane, W0)
-    rows_x_sent(qplane, Q0)
-    rows_x_sent(woplane, O0)
+    rows_first_sent(wplane, W0, 0)
+    rows_first_sent(qplane, Q0, 0)
+    rows_first_sent(woplane, O0, 1)
 
     def drain(where, carried):
         pair_copy(where, where * 2 + core).wait_send()
@@ -418,7 +442,7 @@
     pl.semaphore_signal(barrier, 1, device_id=sibling, device_id_type=MESH)
     pl.semaphore_wait(barrier, 4)
     copies = []
-    for offset in (1, 2, 3):
+    for offset in (2, 1, 3):
         peer = lax.rem(x + offset, RING)
         one = pltpu.make_async_remote_copy(
             src_ref=attended.at[peer], dst_ref=held.at[x], send_sem=send.at[offset - 1],
@@ -439,7 +463,7 @@
         device_id=sibling, device_id_type=MESH,
     ).wait_recv()
     for j in (0, 1):
-        wo_all[384 * j:384 * (j + 1), :] = in_order([wo_both.at[0], wo_both.at[1]], j).astype(BF16)
+        wo_all[384 * j:384 * (j + 1), :] = in_order([wo_both.at[0], wo_both.at[1]], j, True).astype(BF16)
 
     def product(peer, block):
         summed = jnp.concatenate(
@@ -449,14 +473,14 @@
         return lax.dot_general(summed, wo_all[rows, :], TN, preferred_element_type=F32)
 
     numerator = product(x, attended[x])
-    for offset in (1, 2, 3):
+    for offset in (1, 3, 2):
         peer = lax.rem(x + 4 - offset, RING)
         pltpu.make_async_remote_copy(
             src_ref=attended.at[peer], dst_ref=held.at[peer], send_sem=send.at[offset - 1],
             recv_sem=recv.at[offset - 1], device_id=device(peer, z, core), device_id_type=MESH,
         ).wait_recv()
         numerator += product(peer, held[peer])
-    out[0] = (numerator / total[0:1, 0:1]).astype(BF16)
+    out[0] = (numerator * (1.0 / total[0:1, 0:1])).astype(BF16)
     for one in copies:
         one.wait_send()
 
@@ -490,8 +514,8 @@
             pltpu.VMEM((2, 8), I32),
             pltpu.VMEM((2, 8), I32),
             pltpu.VMEM((PLANE, SEQ, D), BF16),
-            pltpu.VMEM((3, 3 * WIDE, 128), BF16),
-            pltpu.VMEM((2, 3, 3 * WIDE, 128), BF16),
+            pltpu.VMEM((2, 3 * WIDE, 128), BF16),
+            pltpu.VMEM((2, 2, 3 * WIDE, 128), BF16),
             pltpu.VMEM((RING, ROWS, 2 * WIDE), BF16),
             pltpu.VMEM((RING, ROWS, 256), BF16),
             pltpu.VMEM((2, RING, RING, ROWS, 2 * WIDE), BF16),

time: 53.6 us -> 52.8 us (0.985)
  Pallas kernels: 52.1 us -> 51.3 us
    pallas_call x1, Pallas kernels: 38.2 us -> 37.2 us  [shards(): pl.pallas_call(gather_kernel, out_shape=(jax.ShapeDtypeStruct((2 * PLANE,...]
where the time goes in v5:
time: 52.8 us; the launch traced here: 52.7 us
  Pallas kernels  51.3 us (97%)
  local copies, waits for them, and re-layouts  0.72 us (1%)
  between operations  0.67 us (1%)
    pallas_call x1, Pallas kernels, shards(): pl.pallas_call(gather_kernel, out_shape=(jax.ShapeDtypeStruct((2 * PLANE,...  37.2 us
    pallas_call x1, Pallas kernels, shards(): pl.pallas_call(output_kernel, out_shape=jax.ShapeDtypeStruct((1, SEQ, D),...  7.54 us
    pallas_call x1, Pallas kernels, shards(): pl.pallas_call(attend_kernel, out_shape=jax.ShapeDtypeStruct((RING, WIDE...  6.63 us

profile of v5, /device:TPU:1, one launch (start us, length us, event | category | flops | bytes accessed | tf_op | source)
XLA Modules:
  0.0 52.7 jit_solution(9576278661637395618)
XLA Ops:
  0.7 37.2 %gather_project.1 = (bf16[32,384,192]{2,1,0:T(8,128)(2,1)S(1)}, bf16[4,128,384]{2,1,0:T(8,128)(2,1)S(1)}, bf16[4,64,192]{2,1,0:T(8,128)(2,1)S(1)}, s32[8,128]{1,...) custom-call(bf16[1,192,768]{2,1,0:T(8,128)(2,1)} %tok_h.1, f32[768]{0:T(1024)} %gain_h.1, ...), custom_call_target="tpu_custom_call" | custom-call | tf_op jit(solution)/shard_map/gather_project/pallas_call | solution.py:494
  37.8 6.6 %attend.1.attended = bf16[4,288,128]{2,1,0:T(8,128)(2,1)S(1)} custom-call(s32[8,128]{1,0:T(8,128)S(1)} %get-tuple-element.11.directions, bf16[32,384,192]{2,1,0:T(8,128)(2,1)S(1)} %get-tuple-element.12.kv, bf16[4,128,384]{2,1,0:T(8,128)(2,1)S(1)} %get-tuple-element.13.both, bf16[4,64,192]{2,1,0:T(8,128)(2,1)S(1)} %get-tuple-element.14.third), custom_call_target="tpu_custom_call" | custom-call | tf_op jit(solution)/shard_map/attend/pallas_call | solution.py:542
  44.4 7.5 %exchange_output.1 = bf16[1,192,768]{2,1,0:T(8,128)(2,1)S(1)} custom-call(bf16[4,288,128]{2,1,0:T(8,128)(2,1)S(1)} %attend.1.attended, bf16[2,4,4,24,768]{4,3,2,1,0:T(8,128)(2,1)S(1)} %get-tuple-element.15.woplane, f32[8,128]{1,0:T(8,128)S(1)} %get-tuple-element.16.total), custom_call_target="tpu_custom_call" | custom-call | tf_op jit(solution)/shard_map/exchange_output/pallas_call | solution.py:553
  52.0 0.7 %copy.13 = bf16[1,192,768]{2,1,0:T(8,128)(2,1)} copy(bf16[1,192,768]{2,1,0:T(8,128)(2,1)S(1)} %exchange_output.1) | data formatting | bytes 589824

commit v6 on v5

--- a/solution.py
+++ b/solution.py
@@ -274,8 +274,8 @@
     ring_start(0, 1)
     rows_first(woplane, O0, None, 1)
     rows_second(wplane, W0, 0)
+    ring_start(1, 1)
     rows_second(qplane, Q0, 0)
-    ring_start(1, 1)
     lists_z(L0)
     ring_pass(0, 0)
     ring_pass(1, 0)
@@ -361,10 +361,10 @@
     ring_pass(2, 1)
     project(2, lambda i: (1 + 2 * i, 2))
     take(2)
+    take(3)
     ring_end(2, 0)
     ring_end(2, 1)
     project(1, lambda i: (i + 2, i + 2))
-    take(3)
 
     for offset in (1, 2, 3):
         arrived(woplane.at[core, turn(y, 4 - offset)], O0 + 5 + offset)

time: 52.8 us -> 53.8 us (1.019); the launches traced: 52.7 us -> 53.2 us
    pallas_call x1, Pallas kernels: 7.54 us -> 8.59 us  [shards(): pl.pallas_call(output_kernel, out_shape=jax.ShapeDtypeStruct((1, SEQ, D),...]
    pallas_call x1, Pallas kernels: 37.2 us -> 36.6 us  [shards(): pl.pallas_call(gather_kernel, out_shape=(jax.ShapeDtypeStruct((2 * PLANE,...]
where the time goes in v6:
time: 53.8 us; the launch traced here: 53.2 us
  Pallas kernels  51.8 us (96%)
  local copies, waits for them, and re-layouts  0.72 us (1%)
  between operations  0.67 us (1%)
    pallas_call x1, Pallas kernels, shards(): pl.pallas_call(gather_kernel, out_shape=(jax.ShapeDtypeStruct((2 * PLANE,...  36.6 us
    pallas_call x1, Pallas kernels, shards(): pl.pallas_call(output_kernel, out_shape=jax.ShapeDtypeStruct((1, SEQ, D),...  8.59 us
    pallas_call x1, Pallas kernels, shards(): pl.pallas_call(attend_kernel, out_shape=jax.ShapeDtypeStruct((RING, WIDE...  6.62 us

profile of v6, /device:TPU:1, one launch (start us, length us, event | category | flops | bytes accessed | tf_op | source)
XLA Modules:
  0.0 53.2 jit_solution(6555209875137989806)
XLA Ops:
  0.7 36.6 %gather_project.1 = (bf16[32,384,192]{2,1,0:T(8,128)(2,1)S(1)}, bf16[4,128,384]{2,1,0:T(8,128)(2,1)S(1)}, bf16[4,64,192]{2,1,0:T(8,128)(2,1)S(1)}, s32[8,128]{1,...) custom-call(bf16[1,192,768]{2,1,0:T(8,128)(2,1)} %tok_h.1, f32[768]{0:T(1024)} %gain_h.1, ...), custom_call_target="tpu_custom_call" | custom-call | tf_op jit(solution)/shard_map/gather_project/pallas_call | solution.py:494
  37.2 6.6 %attend.1.attended = bf16[4,288,128]{2,1,0:T(8,128)(2,1)S(1)} custom-call(s32[8,128]{1,0:T(8,128)S(1)} %get-tuple-element.11.directions, bf16[32,384,192]{2,1,0:T(8,128)(2,1)S(1)} %get-tuple-element.12.kv, bf16[4,128,384]{2,1,0:T(8,128)(2,1)S(1)} %get-tuple-element.13.both, bf16[4,64,192]{2,1,0:T(8,128)(2,1)S(1)} %get-tuple-element.14.third), custom_call_target="tpu_custom_call" | custom-call | tf_op jit(solution)/shard_map/attend/pallas_call | solution.py:542
  43.9 8.6 %exchange_output.1 = bf16[1,192,768]{2,1,0:T(8,128)(2,1)S(1)} custom-call(bf16[4,288,128]{2,1,0:T(8,128)(2,1)S(1)} %attend.1.attended, bf16[2,4,4,24,768]{4,3,2,1,0:T(8,128)(2,1)S(1)} %get-tuple-element.15.woplane, f32[8,128]{1,0:T(8,128)S(1)} %get-tuple-element.16.total), custom_call_target="tpu_custom_call" | custom-call | tf_op jit(solution)/shard_map/exchange_output/pallas_call | solution.py:553
  52.5 0.7 %copy.13 = bf16[1,192,768]{2,1,0:T(8,128)(2,1)} copy(bf16[1,192,768]{2,1,0:T(8,128)(2,1)S(1)} %exchange_output.1) | data formatting | bytes 589824

commit v7 on v6

--- a/solution.py
+++ b/solution.py
@@ -284,10 +284,10 @@
     ring_pass(1, 1)
     ring_pass(0, 1)
     tokens_pass(1)
-    rows_y(qplane, Q0, 0)
     ring_end(1, 0)
     ring_start(2, 0)
     rows_across(wplane, W0)
+    rows_y(qplane, Q0, 0)
     ring_end(1, 1)
     ring_start(2, 1)
     lists_across(L0)

time: 53.8 us -> 54.7 us (1.017); the launches traced: 53.2 us -> 55.1 us
  Pallas kernels: 51.8 us -> 53.8 us
    pallas_call x1, Pallas kernels: 36.6 us -> 38.1 us  [shards(): pl.pallas_call(gather_kernel, out_shape=(jax.ShapeDtypeStruct((2 * PLANE,...]
    pallas_call x1, Pallas kernels: 6.62 us -> 7.79 us  [shards(): pl.pallas_call(attend_kernel, out_shape=jax.ShapeDtypeStruct((RING, WIDE...]
    pallas_call x1, Pallas kernels: 8.59 us -> 7.85 us  [shards(): pl.pallas_call(output_kernel, out_shape=jax.ShapeDtypeStruct((1, SEQ, D),...]
where the time goes in v7:
time: 54.7 us; the launch traced here: 55.1 us
  Pallas kernels  53.8 us (98%)
  local copies, waits for them, and re-layouts  0.72 us (1%)
  between operations  0.67 us (1%)
    pallas_call x1, Pallas kernels, shards(): pl.pallas_call(gather_kernel, out_shape=(jax.ShapeDtypeStruct((2 * PLANE,...  38.1 us
    pallas_call x1, Pallas kernels, shards(): pl.pallas_call(output_kernel, out_shape=jax.ShapeDtypeStruct((1, SEQ, D),...  7.85 us
    pallas_call x1, Pallas kernels, shards(): pl.pallas_call(attend_kernel, out_shape=jax.ShapeDtypeStruct((RING, WIDE...  7.79 us

profile of v7, /device:TPU:1, one launch (start us, length us, event | category | flops | bytes accessed | tf_op | source)
XLA Modules:
  0.0 55.1 jit_solution(8235846297915912603)
XLA Ops:
  0.7 38.1 %gather_project.1 = (bf16[32,384,192]{2,1,0:T(8,128)(2,1)S(1)}, bf16[4,128,384]{2,1,0:T(8,128)(2,1)S(1)}, bf16[4,64,192]{2,1,0:T(8,128)(2,1)S(1)}, s32[8,128]{1,...) custom-call(bf16[1,192,768]{2,1,0:T(8,128)(2,1)} %tok_h.1, f32[768]{0:T(1024)} %gain_h.1, ...), custom_call_target="tpu_custom_call" | custom-call | tf_op jit(solution)/shard_map/gather_project/pallas_call | solution.py:494
  38.8 7.8 %attend.1.attended = bf16[4,288,128]{2,1,0:T(8,128)(2,1)S(1)} custom-call(s32[8,128]{1,0:T(8,128)S(1)} %get-tuple-element.11.directions, bf16[32,384,192]{2,1,0:T(8,128)(2,1)S(1)} %get-tuple-element.12.kv, bf16[4,128,384]{2,1,0:T(8,128)(2,1)S(1)} %get-tuple-element.13.both, bf16[4,64,192]{2,1,0:T(8,128)(2,1)S(1)} %get-tuple-element.14.third), custom_call_target="tpu_custom_call" | custom-call | tf_op jit(solution)/shard_map/attend/pallas_call | solution.py:542
  46.6 7.8 %exchange_output.1 = bf16[1,192,768]{2,1,0:T(8,128)(2,1)S(1)} custom-call(bf16[4,288,128]{2,1,0:T(8,128)(2,1)S(1)} %attend.1.attended, bf16[2,4,4,24,768]{4,3,2,1,0:T(8,128)(2,1)S(1)} %get-tuple-element.15.woplane, f32[8,128]{1,0:T(8,128)S(1)} %get-tuple-element.16.total), custom_call_target="tpu_custom_call" | custom-call | tf_op jit(solution)/shard_map/exchange_output/pallas_call | solution.py:553
  54.4 0.7 %copy.13 = bf16[1,192,768]{2,1,0:T(8,128)(2,1)} copy(bf16[1,192,768]{2,1,0:T(8,128)(2,1)S(1)} %exchange_output.1) | data formatting | bytes 589824
